TPU v7x, 128 devices: a whole 4x4x4 slice. The times are simulated.
128 devices in a mesh: group: 4 (over x), tile: 32 (over y, z, core).
Axes of the slice: x: 4, y: 4, z: 4, core: 2. Of those that a mesh axis runs over, the one named last changes fastest.
Arguments:
- velocity_u: float32 [4, 4096, 1024], P('group', 'tile'), may hold values from -6 to 6
- velocity_v: float32 [4, 4096, 1024], P('group', 'tile'), may hold values from -6 to 6
- tracer: float32 [4, 4096, 1024], P('group', 'tile'), may hold values from -6 to 6
- land: int32 [4096, 1024], P('tile'), may hold values 0 or 1
- tile_depth: int32 [256], replicated, may hold values from 1 to 4, 384 in all
- conv_one: bfloat16 [64, 3, 3, 3], replicated, may hold values from -1.25 to 1.25
- bias_one: float32 [64], replicated, may hold values from -3 to 3
- conv_two: bfloat16 [64, 64, 3, 3], replicated, may hold values from -0.25 to 0.25
- bias_two: float32 [64], replicated, may hold values from -3 to 3
- conv_three: bfloat16 [3, 64, 3, 3], replicated, may hold values from -0.25 to 0.25
- bias_three: float32 [3], replicated, may hold values from -3 to 3
Outputs:
- east_two: float32 [4, 4096, 1024], P('group', 'tile')
- north_two: float32 [4, 4096, 1024], P('group', 'tile')
- tracer_one: float32 [4, 4096, 1024], P('group', 'tile')
Inputs may be any that keep to these rules, and one draw needn't show every extreme that they name: `land`: 1 marks water. `tile_depth`: the entries sum to exactly 384; some column is 4 levels deep.
All inputs are finite; a program needn't handle non-finite values. No bound on the sum of `land` on one device may be relied on, other than what follows from the above.
Results may differ from a plain program's by a relative error of at most 0.00083.
Values may be sent and summed in bfloat16 or wider, within the bound.
A program may use at most 128 MiB of HBM per device.

v0:
```python
import jax
import jax.numpy as jnp
from jax import lax
from jax.sharding import PartitionSpec as P

time_step = 0.1
viscosity = 0.5
diffusivity = 0.5
eddy_gain = 0.5
coriolis_base = 0.2
coriolis_slope = 0.6


def extended_2(block, sides, width):
    for axis, dim in sides:
        count = lax.axis_size(axis)
        forward = [(i, i + 1) for i in range(count - 1)]
        backward = [(target, source) for source, target in forward]
        low = lax.ppermute(
            lax.slice_in_dim(block, block.shape[dim] - width, None, axis=dim), axis, forward
        )
        high = lax.ppermute(lax.slice_in_dim(block, 0, width, axis=dim), axis, backward)
        block = jnp.concatenate([low, block, high], axis=dim)
    return block


def east_diff(field):
    return 0.5 * (field[..., 2:, 1:-1] - field[..., :-2, 1:-1])


def north_diff(field):
    return 0.5 * (field[..., 1:-1, 2:] - field[..., 1:-1, :-2])


def laplace(field):
    return (
        field[..., 2:, 1:-1]
        + field[..., :-2, 1:-1]
        + field[..., 1:-1, 2:]
        + field[..., 1:-1, :-2]
        - 4.0 * field[..., 1:-1, 1:-1]
    )


def advance(padded_east, padded_north, padded_tracer, active, coriolis):
    inner_east = padded_east[..., 1:-1, 1:-1]
    inner_north = padded_north[..., 1:-1, 1:-1]
    inner_tracer = padded_tracer[..., 1:-1, 1:-1]
    grad_east = east_diff(padded_tracer)
    grad_north = north_diff(padded_tracer)
    new_east = inner_east + time_step * active * (
        coriolis * inner_north - grad_east + viscosity * laplace(padded_east)
    )
    new_north = inner_north + time_step * active * (
        -coriolis * inner_east - grad_north + viscosity * laplace(padded_north)
    )
    new_tracer = inner_tracer + time_step * active * (
        -(inner_east * grad_east + inner_north * grad_north) + diffusivity * laplace(padded_tracer)
    )
    return (new_east, new_north, new_tracer)


def latitude(first_row, row_count, total_rows):
    places = (first_row + jnp.arange(row_count, dtype=jnp.int32)).astype(jnp.float32)
    return (coriolis_base + coriolis_slope * (places + 0.5) / total_rows)[:, None]


def convolve(source, kernel):
    return lax.conv_general_dilated(
        source,
        kernel,
        (1, 1),
        "VALID",
        dimension_numbers=("NCHW", "OIHW", "NCHW"),
        preferred_element_type=jnp.float32,
    )


def make_closure(conv_one, bias_one, conv_two, bias_two, conv_three, bias_three):

    def closure(window):
        hidden_one = jax.nn.silu(
            convolve(window[None], conv_one) + bias_one[None, :, None, None]
        ).astype(jnp.bfloat16)
        hidden_two = jax.nn.silu(
            convolve(hidden_one, conv_two) + bias_two[None, :, None, None]
        ).astype(jnp.bfloat16)
        return (convolve(hidden_two, conv_three) + bias_three[None, :, None, None]).astype(
            jnp.bfloat16
        )[0]

    return closure


def body(
    velocity_u,
    velocity_v,
    tracer,
    land,
    tile_depth,
    conv_one,
    bias_one,
    conv_two,
    bias_two,
    conv_three,
    bias_three,
):
    levels_here, rows, cols = velocity_u.shape
    across = cols // rows
    group_index = lax.axis_index("group")
    tile_index = lax.axis_index("tile")
    group_count = lax.axis_size("group")
    tile_count = lax.axis_size("tile")
    total_rows = rows * tile_count
    depth_grid = tile_depth.reshape(tile_count, across)
    my_depth = lax.dynamic_index_in_dim(depth_grid, tile_index, 0, keepdims=False)
    my_levels = group_index * levels_here + jnp.arange(levels_here, dtype=jnp.int32)
    wet_tiles = my_levels[:, None] < my_depth[None, :]
    wet_cells = jnp.repeat(wet_tiles, rows, axis=1)
    active = ((land == 1)[None] & wet_cells[:, None, :]).astype(jnp.float32)
    stacked = jnp.stack([velocity_u, velocity_v, tracer])
    extended = extended_2(stacked, (("tile", 2),), 1)
    extended = jnp.pad(extended, ((0, 0), (0, 0), (0, 0), (1, 1)))
    coriolis = latitude(tile_index * rows, rows, total_rows)
    east_one, north_one, tracer_one = advance(
        extended[0], extended[1], extended[2], active, coriolis
    )
    features = (jnp.stack([east_one, north_one, tracer_one], axis=1) * active[:, None]).astype(
        jnp.bfloat16
    )
    framed = extended_2(features, (("tile", 2),), 3)
    framed = jnp.pad(framed, ((0, 0), (0, 0), (0, 0), (3, 3)))
    windows = jnp.stack(
        [framed[:, :, :, column * rows : column * rows + rows + 6] for column in range(across)],
        axis=1,
    )
    windows = windows.reshape((levels_here * across,) + windows.shape[2:])
    wet_flat = wet_tiles.reshape(-1)
    closure = make_closure(conv_one, bias_one, conv_two, bias_two, conv_three, bias_three)
    level_table = (
        jnp.arange(group_count, dtype=jnp.int32)[:, None] * levels_here
        + jnp.arange(levels_here, dtype=jnp.int32)[None, :]
    )
    wet_count = wet_flat.astype(jnp.int32)
    slot_count = levels_here * across // group_count
    row_counts = jnp.sum(
        (level_table[:, :, None] < my_depth[None, None, :]).astype(jnp.int32), axis=(1, 2)
    )
    row_starts = jnp.cumsum(row_counts) - row_counts
    row_ends = row_starts + row_counts
    first_rank = row_starts[group_index]
    ranks = first_rank + jnp.cumsum(wet_count) - wet_count
    owners = ranks % group_count
    slot_of = (ranks - first_rank) // group_count
    targets = jnp.where(wet_flat, owners * slot_count + slot_of, group_count * slot_count)
    outgoing = (
        jnp.zeros((group_count * slot_count,) + windows.shape[1:], jnp.bfloat16)
        .at[targets]
        .set(windows, mode="drop")
    )
    outgoing = outgoing.reshape((group_count, slot_count) + windows.shape[1:])
    arriving = lax.all_to_all(outgoing, "group", split_axis=0, concat_axis=0, tiled=True)

    def count_below(limit):
        return (limit - group_index + group_count - 1) // group_count

    received = count_below(row_ends) - count_below(row_starts)
    filled = (jnp.arange(slot_count, dtype=jnp.int32)[None, :] < received[:, None]).reshape(-1)
    ranked = jnp.argsort(1 - filled.astype(jnp.int32), stable=True)
    arrivals = jnp.sum(received)
    flat_in = arriving.reshape((group_count * slot_count,) + windows.shape[1:])
    components = conv_three.shape[0]

    def evaluate(step, outputs):
        position = ranked[step]
        window_in = lax.dynamic_index_in_dim(flat_in, position, 0, keepdims=False)
        return lax.dynamic_update_index_in_dim(outputs, closure(window_in), position, 0)

    outputs = lax.fori_loop(
        0,
        arrivals,
        evaluate,
        jnp.zeros((group_count * slot_count, components, rows, rows), jnp.bfloat16),
    )
    returning = outputs.reshape(group_count, slot_count, components, rows, rows)
    landed = lax.all_to_all(returning, "group", split_axis=0, concat_axis=0, tiled=True)
    landed = landed.reshape(group_count * slot_count, components, rows, rows)
    picked = landed[jnp.where(wet_flat, owners * slot_count + slot_of, 0)]
    mine = jnp.where(wet_flat[:, None, None, None], picked, jnp.zeros_like(picked))
    components = mine.shape[1]
    stress = mine.reshape(levels_here, across, components, rows, rows).transpose(0, 2, 3, 1, 4)
    stress = stress.reshape(levels_here, components, rows, cols)
    masked = (stress.astype(jnp.float32) * active[:, None]).astype(jnp.bfloat16)
    framed_stress = extended_2(masked, (("tile", 2),), 1)
    framed_stress = jnp.pad(framed_stress.astype(jnp.float32), ((0, 0), (0, 0), (0, 0), (1, 1)))
    push_east = east_diff(framed_stress[:, 0]) + north_diff(framed_stress[:, 1])
    push_north = east_diff(framed_stress[:, 1]) + north_diff(framed_stress[:, 2])
    east_two = east_one + eddy_gain * active * push_east
    north_two = north_one + eddy_gain * active * push_north
    return (east_two, north_two, tracer_one)


def solution(mesh):
    in_specs = (
        P("group", "tile", None),
        P("group", "tile", None),
        P("group", "tile", None),
        P("tile", None),
        P(),
        P(),
        P(),
        P(),
        P(),
        P(),
        P(),
    )
    out_specs = (P("group", "tile", None), P("group", "tile", None), P("group", "tile", None))
    return jax.shard_map(body, mesh=mesh, in_specs=in_specs, out_specs=out_specs, check_vma=False)
```

profile of v0, /device:TPU:49, one launch (start us, length us, event | category | flops | bytes accessed | tf_op | source)
XLA Modules:
  0.0 824.2 jit_solution(10441029040377337368)
XLA Ops:
  5.5 4.1 collective-permute-start
  19.1 3.6 select_maximum_fusion
  26.3 3.6 collective-permute-start.2
  42.1 4.1 all-to-all-start
  47.4 19.8 %all-to-all-done = bf16[4,2,3,134,134]{4,1,3,2,0:T(2,128)(2,1)S(1)} async-done(((bf16[4,2,3,134,134]{4,1,3,2,0:T(2,128)(2,1)}), bf16[4,2,3,134,134]{4,1,3,2,0:T(2,128)(2,1)S(1)}, u32[]{:S(2)}, u32[]{:S(2)}) %all-to-all-start) | async-done | bytes 861920 | tf_op jit(solution)/shard_map/all_to_all | solution.py:162
  69.9 439.8 %while.10 = (s32[]{:T(128)}, bf16[8,3,128,128]{2,3,1,0:T(8,128)(2,1)}, s32[]{:T(128)}, s32[8]{0:T(128)S(1)}, bf16[8,3,134,134]{2,3,1,0:T(8,128)(2,1)S(1)}, /*ind...) while((s32[]{:T(128)}, ...), condition=%wide.region_7.8_spmd, body=%wide.region_6.7_spmd.sunk | while | flops 1458590720 | bytes 20074620 | solution.py:179
  93.2 10.2 %copy.168 = bf16[3,134,1,8,17]{3,0,4,1,2:T(4,128)(2,1)S(1)} copy(bf16[3,134,1,8,17]{1,4,3,0,2:T(8,128)(2,1)S(1)} %reshape.508) | data formatting | bytes 218688 | tf_op jit(solution)/shard_map/while/body/conv_general_dilated | solution.py:69
  103.6 9.4 %select_bitcast_fusion.4 = bf16[132,1,8,17,64]{4,2,3,0,1:T(8,128)(2,1)S(1)} fusion(f32[64]{0:T(128)S(1)} %get-tuple-element.313, pred[8,17]{0,1:T(8,128)(4,1)S(1)} %get-tuple-element.322, bf16[64,3,3,3]{0,1,3,2:T(4,128)(2,1)S(1)} %get-tuple-element.312, bf16[3,134,1,7,2]{3,0,4,1,2:T(4,128)(2,1)S(1)} %slice.364, ...), kind=kOutput, calls=%fused_computation.22.clone.1 | convolution fusion | flops 71600160 | bytes 2422304 | tf_op jit(solution)/shard_map/while/body/conv_general_dilated | solution.py:69
  113.2 12.1 %select_bitcast_fusion.5 = bf16[130,1,8,17,64]{4,2,3,0,1:T(8,128)(2,1)S(1)} fusion(f32[64]{0:T(128)S(1)} %get-tuple-element.315, pred[8,17]{0,1:T(8,128)(4,1)S(1)} %get-tuple-element.321, bf16[64,64,3,3]{1,0,3,2:T(8,128)(2,1)S(1)} %get-tuple-element.314, bf16[132,1,7,2,64]{4,2,3,0,1:T(8,128)(2,1)S(1)} %slice.365, ...), kind=kOutput, calls=%fused_computation.23.clone.1 | convolution fusion | flops 1319136256 | bytes 4871560 | tf_op jit(solution)/shard_map/while/body/conv_general_dilated | solution.py:69
  125.4 99.3 %fusion.111 = f32[128,8,17,3]{1,3,2,0:T(4,128)} fusion(bf16[3,64,3,3]{1,0,3,2:T(4,128)(2,1)S(1)} %get-tuple-element.316, bf16[130,1,7,2,64]{4,2,3,0,1:T(8,128)(2,1)S(1)} %slice.366, bf16[130,1,8,17,64]{4,2,3,0,1:T(8,128)(2,1)S(1)} %select_bitcast_fusion.5), kind=kOutput, calls=%fused_computation.18.clone.1 | convolution fusion | flops 67749888 | bytes 2708352 | tf_op jit(solution)/shard_map/while/body/conv_general_dilated | solution.py:69
  224.7 3.7 copy.169
  233.0 10.2 %copy.168 = bf16[3,134,1,8,17]{3,0,4,1,2:T(4,128)(2,1)S(1)} copy(bf16[3,134,1,8,17]{1,4,3,0,2:T(8,128)(2,1)S(1)} %reshape.508) | data formatting | bytes 218688 | tf_op jit(solution)/shard_map/while/body/conv_general_dilated | solution.py:69
  243.4 9.4 %select_bitcast_fusion.4 = bf16[132,1,8,17,64]{4,2,3,0,1:T(8,128)(2,1)S(1)} fusion(f32[64]{0:T(128)S(1)} %get-tuple-element.313, pred[8,17]{0,1:T(8,128)(4,1)S(1)} %get-tuple-element.322, bf16[64,3,3,3]{0,1,3,2:T(4,128)(2,1)S(1)} %get-tuple-element.312, bf16[3,134,1,7,2]{3,0,4,1,2:T(4,128)(2,1)S(1)} %slice.364, ...), kind=kOutput, calls=%fused_computation.22.clone.1 | convolution fusion | flops 71600160 | bytes 2422304 | tf_op jit(solution)/shard_map/while/body/conv_general_dilated | solution.py:69
  253.0 12.1 %select_bitcast_fusion.5 = bf16[130,1,8,17,64]{4,2,3,0,1:T(8,128)(2,1)S(1)} fusion(f32[64]{0:T(128)S(1)} %get-tuple-element.315, pred[8,17]{0,1:T(8,128)(4,1)S(1)} %get-tuple-element.321, bf16[64,64,3,3]{1,0,3,2:T(8,128)(2,1)S(1)} %get-tuple-element.314, bf16[132,1,7,2,64]{4,2,3,0,1:T(8,128)(2,1)S(1)} %slice.365, ...), kind=kOutput, calls=%fused_computation.23.clone.1 | convolution fusion | flops 1319136256 | bytes 4871560 | tf_op jit(solution)/shard_map/while/body/conv_general_dilated | solution.py:69
  265.2 99.3 %fusion.111 = f32[128,8,17,3]{1,3,2,0:T(4,128)} fusion(bf16[3,64,3,3]{1,0,3,2:T(4,128)(2,1)S(1)} %get-tuple-element.316, bf16[130,1,7,2,64]{4,2,3,0,1:T(8,128)(2,1)S(1)} %slice.366, bf16[130,1,8,17,64]{4,2,3,0,1:T(8,128)(2,1)S(1)} %select_bitcast_fusion.5), kind=kOutput, calls=%fused_computation.18.clone.1 | convolution fusion | flops 67749888 | bytes 2708352 | tf_op jit(solution)/shard_map/while/body/conv_general_dilated | solution.py:69
  364.5 3.7 copy.169
  372.8 10.2 %copy.168 = bf16[3,134,1,8,17]{3,0,4,1,2:T(4,128)(2,1)S(1)} copy(bf16[3,134,1,8,17]{1,4,3,0,2:T(8,128)(2,1)S(1)} %reshape.508) | data formatting | bytes 218688 | tf_op jit(solution)/shard_map/while/body/conv_general_dilated | solution.py:69
  383.2 9.4 %select_bitcast_fusion.4 = bf16[132,1,8,17,64]{4,2,3,0,1:T(8,128)(2,1)S(1)} fusion(f32[64]{0:T(128)S(1)} %get-tuple-element.313, pred[8,17]{0,1:T(8,128)(4,1)S(1)} %get-tuple-element.322, bf16[64,3,3,3]{0,1,3,2:T(4,128)(2,1)S(1)} %get-tuple-element.312, bf16[3,134,1,7,2]{3,0,4,1,2:T(4,128)(2,1)S(1)} %slice.364, ...), kind=kOutput, calls=%fused_computation.22.clone.1 | convolution fusion | flops 71600160 | bytes 2422304 | tf_op jit(solution)/shard_map/while/body/conv_general_dilated | solution.py:69
  392.7 12.1 %select_bitcast_fusion.5 = bf16[130,1,8,17,64]{4,2,3,0,1:T(8,128)(2,1)S(1)} fusion(f32[64]{0:T(128)S(1)} %get-tuple-element.315, pred[8,17]{0,1:T(8,128)(4,1)S(1)} %get-tuple-element.321, bf16[64,64,3,3]{1,0,3,2:T(8,128)(2,1)S(1)} %get-tuple-element.314, bf16[132,1,7,2,64]{4,2,3,0,1:T(8,128)(2,1)S(1)} %slice.365, ...), kind=kOutput, calls=%fused_computation.23.clone.1 | convolution fusion | flops 1319136256 | bytes 4871560 | tf_op jit(solution)/shard_map/while/body/conv_general_dilated | solution.py:69
  405.0 99.3 %fusion.111 = f32[128,8,17,3]{1,3,2,0:T(4,128)} fusion(bf16[3,64,3,3]{1,0,3,2:T(4,128)(2,1)S(1)} %get-tuple-element.316, bf16[130,1,7,2,64]{4,2,3,0,1:T(8,128)(2,1)S(1)} %slice.366, bf16[130,1,8,17,64]{4,2,3,0,1:T(8,128)(2,1)S(1)} %select_bitcast_fusion.5), kind=kOutput, calls=%fused_computation.18.clone.1 | convolution fusion | flops 67749888 | bytes 2708352 | tf_op jit(solution)/shard_map/while/body/conv_general_dilated | solution.py:69
  504.2 3.7 copy.169
  512.1 3.6 all-to-all-start.1
  516.8 11.4 %all-to-all-done.1 = bf16[4,2,3,128,128]{4,3,2,1,0:T(8,128)(2,1)S(1)} async-done(((bf16[4,2,3,128,128]{4,3,2,1,0:T(8,128)(2,1)}), bf16[4,2,3,128,128]{4,3,2,1,0:T(8,128)(2,1)S(1)}, u32[]{:S(2)}, u32[]{:S(2)}) %all-to-all-start.1) | async-done | bytes 786464 | tf_op jit(solution)/shard_map/all_to_all | solution.py:186
  540.6 277.4 %collective-permute-done.5 = bf16[1,3,1,1024]{3,1,2,0:T(4,128)(2,1)S(1)} collective-permute-done((bf16[1,3,1,1024]{3,1,2,0:T(4,128)(2,1)S(1)}, bf16[1,3,1,1024]{3,1,2,0:T(4,128)(2,1)S(1)}, u32[]{:S(2)}, u32[]{:S(2)}) %collective-permute-start.5) | collective-permute-done | bytes 6176 | tf_op jit(solution)/shard_map/ppermute | solution.py:22
  (181 shorter events, 61.6 us)
Async XLA Ops:
  5.0 7.0 copy-start.24
  5.5 11.4 %collective-permute-start = (f32[3,1,1,1024]{3,2,1,0:T(1,128)S(1)}, f32[3,1,1,1024]{3,2,1,0:T(1,128)S(1)}, u32[]{:S(2)}, u32[]{:S(2)}) collective-permute-start(f32[3,1,1,1024]{3,2,1,0:T(1,128)S(1)} %copy.139), channel_id=1, source_target_pairs={{0,1},{1,2},{2,3},{3,4},{4,5},{5,6},{6,7},{7,8},{8,9},{9,10},{10,1... | collective-permute-start | bytes 36872 | tf_op jit(solution)/shard_map/ppermute | solution.py:19
  10.1 7.4 collective-permute-start.1
  12.1 20.0 %copy-start.21 = (pred[1,8]{1,0:T(4,128)(4,1)}, pred[1,8]{1,0:T(4,128)(4,1)S(1)}, u32[]{:S(2)}) copy-start(pred[1,8]{1,0:T(4,128)(4,1)S(1)} %get-tuple-element.183) | copy-start | bytes 28
  13.5 5.7 copy-start.5
  13.5 5.7 copy-start.7
  14.9 9.4 %copy-start.15 = (pred[128,1024]{0,1:T(8,128)(4,1)}, pred[128,1024]{0,1:T(8,128)(4,1)S(1)}, u32[]{:S(2)}) copy-start(pred[128,1024]{0,1:T(8,128)(4,1)S(1)} %get-tuple-element.181) | copy-start | bytes 393220
  14.9 10.3 %copy-start = (f32[128,1024]{0,1:T(8,128)}, f32[128,1024]{0,1:T(8,128)S(1)}, u32[]{:S(2)}) copy-start(f32[128,1024]{0,1:T(8,128)S(1)} %get-tuple-element.180) | copy-start | bytes 1572868
  26.3 5.9 collective-permute-start.2
  30.2 5.1 collective-permute-start.3
  42.1 25.1 %all-to-all-start = ((bf16[4,2,3,134,134]{4,1,3,2,0:T(2,128)(2,1)}), bf16[4,2,3,134,134]{4,1,3,2,0:T(2,128)(2,1)S(1)}, u32[]{:S(2)}, u32[]{:S(2)}) async-start(bf16[4,2,3,134,134]{4,1,3,2,0:T(2,128)(2,1)} %copy.149), calls=%async_computation | async-start | bytes 3293184 | tf_op jit(solution)/shard_map/all_to_all | solution.py:162
  46.1 23.7 %copy-start.18 = (f32[3]{0:T(128)S(1)}, f32[3]{0:T(128)}, u32[]{:S(2)}) copy-start(f32[3]{0:T(128)} %param.23) | copy-start | bytes 40
  46.1 23.7 %copy-start.25 = (bf16[64,64,3,3]{1,0,3,2:T(8,128)(2,1)S(1)}, bf16[64,64,3,3]{1,0,3,2:T(8,128)(2,1)}, u32[]{:S(2)}) copy-start(bf16[64,64,3,3]{1,0,3,2:T(8,128)(2,1)} %param.20) | copy-start | bytes 221188
  46.1 23.7 %copy-start.26 = (f32[64]{0:T(128)S(1)}, f32[64]{0:T(128)}, u32[]{:S(2)}) copy-start(f32[64]{0:T(128)} %param.19) | copy-start | bytes 772
  46.1 23.7 %copy-start.27 = (f32[64]{0:T(128)S(1)}, f32[64]{0:T(128)}, u32[]{:S(2)}) copy-start(f32[64]{0:T(128)} %param.21) | copy-start | bytes 772
  46.2 23.7 %copy-start.28 = (pred[8,17]{0,1:T(8,128)(4,1)S(1)}, pred[8,17]{0,1:T(8,128)(4,1)}, u32[]{:S(2)}) copy-start(pred[8,17]{0,1:T(8,128)(4,1)} %constant.371) | copy-start | bytes 412
  46.2 23.7 %copy-start.29 = (pred[8,17]{0,1:T(8,128)(4,1)S(1)}, pred[8,17]{0,1:T(8,128)(4,1)}, u32[]{:S(2)}) copy-start(pred[8,17]{0,1:T(8,128)(4,1)} %constant.372) | copy-start | bytes 412
  224.7 4.6 copy-start.14
  509.7 6.0 copy-start.23
  509.7 6.0 copy-start.12
  512.1 16.8 %copy-start.22 = (pred[1,8]{1,0:T(4,128)(4,1)S(1)}, pred[1,8]{1,0:T(4,128)(4,1)}, u32[]{:S(2)}) copy-start(pred[1,8]{1,0:T(4,128)(4,1)} %copy-done.21) | copy-start | bytes 28
  512.1 16.1 %all-to-all-start.1 = ((bf16[4,2,3,128,128]{4,3,2,1,0:T(8,128)(2,1)}), bf16[4,2,3,128,128]{4,3,2,1,0:T(8,128)(2,1)S(1)}, u32[]{:S(2)}, u32[]{:S(2)}) async-start(bf16[4,2,3,128,128]{4,3,2,1,0:T(8,128)(2,1)} %copy.154), calls=%async_computation.1 | async-start | bytes 1572864 | tf_op jit(solution)/shard_map/all_to_all | solution.py:186
  535.0 5.1 collective-permute-start.4
  537.3 280.6 %collective-permute-start.5 = (bf16[1,3,1,1024]{3,1,2,0:T(4,128)(2,1)S(1)}, bf16[1,3,1,1024]{3,1,2,0:T(4,128)(2,1)S(1)}, u32[]{:S(2)}, u32[]{:S(2)}) collective-permute-start(bf16[1,3,1,1024]{3,1,2,0:T(4,128)(2,1)S(1)} %copy.158), channel_id=1, source_target_pairs={{1,0},{2,1},{3,2},{4,3},{5,4},{6,5},{7,6},{8,7},{9,8},{10,9},{11,1... | collective-permute-start | bytes 18440 | tf_op jit(solution)/shard_map/ppermute | solution.py:22
  (18 other events, 41.7 us)
where the time goes:
time: 834 us; the launch traced here: 824 us
  matrix products  362 us (43%)
  waiting for transfers between devices  311 us (37%)
  local copies, waits for them, and re-layouts  81.1 us (10%)
  loops' own time  29.2 us (4%)
  starting transfers between devices  23.8 us (3%)
  other arithmetic  14.7 us (2%)
    conv_general_dilated x9, matrix products, convolve(): lax.conv_general_dilated(source, kernel, (1, 1), 'VALID', dimension_numbe...  362 us
    ppermute x3, waiting for transfers between devices, extended_2(): lax.ppermute(lax.slice_in_dim(block, 0, width, axis=dim), axis, backward)  280 us
    conv_general_dilated x12, local copies, waits for them, and re-layouts, convolve(): lax.conv_general_dilated(source, kernel, (1, 1), 'VALID', dimension_numbe...  42.7 us
    another operation x1, loops' own time, body(): lax.fori_loop(0, arrivals, evaluate, jnp.zeros((group_count * slot_count,...  29.2 us
    all_to_all x1, waiting for transfers between devices, body(): lax.all_to_all(outgoing, 'group', split_axis=0, concat_axis=0, tiled=True)  19.8 us
  transfers between devices with their start and end apart: 8, of which 4 were waited for; matrix products, arithmetic and copies ran while one was open for 1% of the time, Pallas kernels for 0%

commit v1 on v0

v1 whole, which is shorter than its diff:
```python
import functools

import jax
import jax.numpy as jnp
import numpy as np
from jax import lax
from jax.experimental import pallas as pl
from jax.experimental.pallas import tpu as pltpu
from jax.sharding import PartitionSpec as P

time_step = 0.1
viscosity = 0.5
diffusivity = 0.5
eddy_gain = 0.5
coriolis_base = 0.2
coriolis_slope = 0.6

bf16 = jnp.bfloat16
f32 = jnp.float32

TS = 128
HALO = 5
ROWS1, ROWS2, ROWS3 = 35, 34, 33
SLAB = 160
USED = 144


def select_in():
    table = np.zeros((80, 256), np.float32)
    for t in range(10):
        for s in range(8):
            table[t * 8 + s, 2 * (9 * s + t)] = 1.0
    return table


def select_out():
    table = np.zeros((2, 2, 160, 256), np.float32)
    for ip in range(2):
        for b in range(2):
            for t in range(9):
                for s in range(8):
                    place = 2 * (9 * s + t) + b
                    if place < 130:
                        table[ip, b, t * 16 + ip * 8 + s, place] = 1.0
    return table


def taps():
    for outer in range(2):
        for inner in range(2):
            for out in range(2):
                k = 2 * outer + inner - out
                if 0 <= k < 3:
                    yield outer, inner, out, k


def build_weights(w1, w2, w3, w1f, w1s, w2s, w3f, w3s):
    w1f[...] = jnp.zeros_like(w1f)
    for q in range(4):
        for dj, dy, b, ky in taps():
            for c in range(3):
                for a in range(2):
                    row = dj * 128 + dy * 48 + c * 16 + 4 + 2 * q + a
                    lane = (a * 2 + b) * 64
                    w1f[q, row : row + 3, lane : lane + 64] = 0.5 * w1[c, ky]
    w1s[...] = w1f[...].astype(bf16)
    w2s[...] = jnp.zeros_like(w2s)
    for di, ai, ao, kx in taps():
        for dj, bi, bo, ky in taps():
            row = (ai * 2 + bi) * 64
            lane = (ao * 2 + bo) * 64
            w2s[di * 2 + dj, row : row + 64, lane : lane + 64] = (0.5 * w2[kx, ky]).astype(bf16)
    w3f[...] = jnp.zeros_like(w3f)
    for di, ai, ao, kx in taps():
        for dj, bi, bo, ky in taps():
            lane = (ai * 2 + bi) * 64
            for c in range(3):
                row = (di * 2 + dj) * 16 + bo * 6 + c * 2 + ao
                w3f[row : row + 1, lane : lane + 64] = w3[c, kx, ky : ky + 1]
    w3s[...] = w3f[...].astype(bf16)


def build_features(meta, depth, u, v, t, land, lo, hi, east, north, tracer, ext, landx, feat, act):
    level, tile = meta[0], meta[1]
    cols = u.shape[1]
    for f, src in enumerate((u, v, t)):
        ext[f, 0:16, :] = jnp.zeros((16, cols), f32)
        ext[f, 144:160, :] = jnp.zeros((16, cols), f32)
        ext[f, 16:144, :] = src[...]
        ext[f, 16 - HALO : 16, :] = lo[f]
        ext[f, 144 : 144 + HALO, :] = hi[f]
    landx[0:16, :] = jnp.zeros((16, cols), f32)
    landx[144:160, :] = jnp.zeros((16, cols), f32)
    landx[16:144, :] = land[...].astype(f32)
    landx[16 - HALO : 16, :] = lo[3]
    landx[144 : 144 + HALO, :] = hi[3]
    lane = lax.broadcasted_iota(jnp.int32, (8, cols), 1)
    row = lax.broadcasted_iota(jnp.int32, (8, cols), 0)
    last = depth.shape[0] // (cols // TS) - 1

    def wet_line(tile_row):
        line = jnp.zeros((8, cols), f32)
        for ty in range(cols // TS):
            wet = (depth[tile_row * (cols // TS) + ty] > level).astype(f32)
            line = jnp.where(lane // TS == ty, wet, line)
        return line

    wet_low = wet_line(jnp.maximum(tile - 1, 0))
    wet_mid = wet_line(tile)
    wet_high = wet_line(jnp.minimum(tile + 1, last))
    rows_all = float((last + 1) * TS)
    zeros = jnp.zeros((8, TS), f32)

    def west(x):
        return jnp.where(lane == 0, 0.0, pltpu.roll(x, 1, 1))

    def east_of(x):
        return jnp.where(lane == cols - 1, 0.0, pltpu.roll(x, cols - 1, 1))

    for k in range(-1, 17):
        base = 8 * k + 16
        wet = wet_low if k < 0 else (wet_high if k > 15 else wet_mid)
        active = jnp.where(landx[base : base + 8, :] == 1.0, wet, 0.0)
        mid = [ext[f, base : base + 8, :] for f in range(3)]
        up = [ext[f, base - 1 : base + 7, :] for f in range(3)]
        down = [ext[f, base + 1 : base + 9, :] for f in range(3)]
        left = [west(x) for x in mid]
        right = [east_of(x) for x in mid]
        lap = [down[f] + up[f] + right[f] + left[f] - 4.0 * mid[f] for f in range(3)]
        grad_east = 0.5 * (down[2] - up[2])
        grad_north = 0.5 * (right[2] - left[2])
        place = (tile * TS + 8 * k + row).astype(f32)
        coriolis = coriolis_base + coriolis_slope * (place + 0.5) / rows_all
        step = time_step * active
        new_east = mid[0] + step * (coriolis * mid[1] - grad_east + viscosity * lap[0])
        new_north = mid[1] + step * (-coriolis * mid[0] - grad_north + viscosity * lap[1])
        new_tracer = mid[2] + step * (
            -(mid[0] * grad_east + mid[1] * grad_north) + diffusivity * lap[2]
        )
        if 0 <= k < 16:
            east[8 * k : 8 * k + 8, :] = new_east
            north[8 * k : 8 * k + 8, :] = new_north
            tracer[8 * k : 8 * k + 8, :] = new_tracer
        q = 8 * k + 8
        for c, new in enumerate((new_east, new_north, new_tracer)):
            wide = jnp.concatenate([new * active, zeros], axis=1)
            feat[0, c, q : q + 8, :] = pltpu.roll(wide, 4, 1)
            feat[1, c, q : q + 8, :] = pltpu.roll(wide, 3, 1)
        act[q : q + 8, :] = pltpu.roll(jnp.concatenate([active, zeros], axis=1), 1, 1)


def silu_half(half):
    return half + half * jnp.tanh(half)


def store_slab(ref, index, value):
    ref[index, 0:USED, :] = value.astype(bf16)
    ref[index, USED:SLAB, :] = pltpu.roll(value[0:16], 15, 0).astype(bf16)


def closure_tile(lane0, sel_in, sel_out, b1, b2, b3, w1s, w2s, w3s, feat, patches, h1, h2, parts, flat):
    for g in range(9):
        halves = []
        for ip in range(2):
            base = 64 * ip + 8 * g
            rows = feat[:, :, base : base + 16, pl.ds(lane0, 256)].reshape(96, 256)
            rows = jnp.concatenate([rows, jnp.zeros((32, 256), f32)], axis=0).astype(bf16)
            got = lax.dot_general(
                sel_in[...], rows, (((1,), (1,)), ((), ())), preferred_element_type=f32
            )
            halves.append(got.reshape(10, 8, 128))
        both = jnp.stack(halves, axis=1).reshape(SLAB, 128)
        patches[g] = both.astype(bf16)
    for q in range(4):
        for g in range(9):
            if 4 * g + q >= ROWS1:
                continue
            lhs = jnp.concatenate([patches[g, 0:USED, :], patches[g, 16:SLAB, :]], axis=1)
            half = jnp.dot(lhs, w1s[q], preferred_element_type=f32) + b1[...]
            store_slab(h1, 4 * g + q, silu_half(half))
    for i in range(0, ROWS2, 2):
        half = b2[...]
        for di in range(2):
            for dj in range(2):
                lhs = h1[i + di : i + di + 2, 16 * dj : 16 * dj + USED, :].reshape(2 * USED, 256)
                half = half + jnp.dot(lhs, w2s[2 * di + dj], preferred_element_type=f32)
        out = silu_half(half)
        store_slab(h2, i, out[0:USED])
        store_slab(h2, i + 1, out[USED:])
    for i in range(ROWS2):
        parts[i] = lax.dot_general(
            w3s[...], h2[i], (((1,), (1,)), ((), ())), preferred_element_type=f32
        )
    for i in range(ROWS3):
        got = (
            parts[i, 0:16, 0:USED]
            + parts[i, 16:32, 16:SLAB]
            + parts[i + 1, 32:48, 0:USED]
            + parts[i + 1, 48:64, 16:SLAB]
        )
        for b in range(2):
            for c in range(3):
                r = b * 6 + c * 2
                flat[b, c, 2 * i : 2 * i + 2, 0:USED] = got[r : r + 2] + b3[c]


def finish_tile(lane0, sel_out, flat, act, east, north):
    for ip in range(2):
        mask = act[8 + 64 * ip - 1 : 8 + 64 * ip + 65, pl.ds(lane0, 256)]
        masked = []
        for c in range(3):
            image = jnp.zeros((72, 256), f32)
            for b in range(2):
                image = image + jnp.dot(
                    flat[b, c].astype(bf16), sel_out[ip, b], preferred_element_type=f32
                )
            masked.append(image[0:66] * mask)
        xx, xy, yy = masked

        def dx(m):
            return 0.5 * (m[2:66, 1:129] - m[0:64, 1:129])

        def dy(m):
            return 0.5 * (m[1:65, 2:130] - m[1:65, 0:128])

        gain = eddy_gain * mask[1:65, 1:129]
        rows = slice(64 * ip, 64 * ip + 64)
        east[rows, pl.ds(lane0, 128)] += gain * (dx(xx) + dy(xy))
        north[rows, pl.ds(lane0, 128)] += gain * (dx(xy) + dy(yy))


def kernel(
    meta, depth, b3, u, v, t, land, lo, hi, w1, b1, w2, b2, w3, sel_in, sel_out,
    east, north, tracer,
    ext, landx, feat, act, w1f, w1s, w2s, w3f, w3s, patches, h1, h2, parts, flat,
):
    build_weights(w1, w2, w3, w1f, w1s, w2s, w3f, w3s)
    build_features(meta, depth, u, v, t, land, lo, hi, east, north, tracer, ext, landx, feat, act)
    flat[...] = jnp.zeros_like(flat)
    across = u.shape[1] // TS

    def column(ty, carry):
        @pl.when(depth[meta[1] * across + ty] > meta[0])
        def _():
            lane0 = pl.multiple_of(ty * TS, TS)
            closure_tile(
                lane0, sel_in, sel_out, b1, b2, b3, w1s, w2s, w3s, feat, patches, h1, h2, parts, flat
            )
            finish_tile(lane0, sel_out, flat, act, east, north)

        return carry

    lax.fori_loop(0, across, column, 0)


def body(u, v, t, land, depth, conv_one, bias_one, conv_two, bias_two, conv_three, bias_three):
    levels, rows, cols = u.shape
    tiles = lax.axis_size("tile")
    fields = jnp.concatenate([u, v, t, land[None].astype(f32)], axis=0)
    forward = [(i, i + 1) for i in range(tiles - 1)]
    backward = [(i + 1, i) for i in range(tiles - 1)]
    lo = lax.ppermute(fields[:, rows - HALO :], "tile", forward)
    hi = lax.ppermute(fields[:, :HALO], "tile", backward)
    meta = jnp.stack([lax.axis_index("group"), lax.axis_index("tile")]).astype(jnp.int32)
    w1 = conv_one.transpose(1, 3, 2, 0).astype(f32)
    w2 = conv_two.transpose(2, 3, 1, 0).astype(f32)
    w3 = conv_three.transpose(0, 2, 3, 1).astype(f32)
    b1 = jnp.tile(0.5 * bias_one, 4)[None]
    b2 = jnp.tile(0.5 * bias_two, 4)[None]
    sel_in = jnp.asarray(select_in(), bf16)
    sel_out = jnp.asarray(select_out(), bf16)
    vmem = pl.BlockSpec(memory_space=pltpu.VMEM)
    smem = pl.BlockSpec(memory_space=pltpu.SMEM)
    wide = cols + TS
    east, north, tracer = pl.pallas_call(
        kernel,
        out_shape=[jax.ShapeDtypeStruct((rows, cols), f32)] * 3,
        in_specs=[smem] * 3 + [vmem] * 13,
        out_specs=[vmem] * 3,
        scratch_shapes=[
            pltpu.VMEM((3, 160, cols), f32),
            pltpu.VMEM((160, cols), f32),
            pltpu.VMEM((2, 3, 144, wide), f32),
            pltpu.VMEM((144, wide), f32),
            pltpu.VMEM((4, 256, 256), f32),
            pltpu.VMEM((4, 256, 256), bf16),
            pltpu.VMEM((4, 256, 256), bf16),
            pltpu.VMEM((64, 256), f32),
            pltpu.VMEM((64, 256), bf16),
            pltpu.VMEM((9, SLAB, 128), bf16),
            pltpu.VMEM((ROWS1 + 1, SLAB, 256), bf16),
            pltpu.VMEM((ROWS2, SLAB, 256), bf16),
            pltpu.VMEM((ROWS2, 64, SLAB), f32),
            pltpu.VMEM((2, 3, 72, SLAB), f32),
        ],
        compiler_params=pltpu.CompilerParams(vmem_limit_bytes=56 * 2**20),
        name="step",
    )(meta, depth, bias_three, u[0], v[0], t[0], land, lo, hi, w1, b1, w2, b2, w3, sel_in, sel_out)
    return east[None], north[None], tracer[None]


def solution(mesh):
    field = P("group", "tile", None)
    in_specs = (field, field, field, P("tile", None)) + (P(),) * 7
    return jax.shard_map(
        body, mesh=mesh, in_specs=in_specs, out_specs=(field,) * 3, check_vma=False
    )
```

time: 834 us -> 67.4 us (0.08)
  the two profiles are of different devices: /device:TPU:49 before, /device:TPU:24 now
where the time goes in v1:
time: 67.4 us; the launch traced here: 67.1 us
  Pallas kernels  49.6 us (74%)
  starting transfers between devices  7.49 us (11%)
  other arithmetic  4.6 us (7%)
  local copies, waits for them, and re-layouts  2.38 us (4%)
  waiting for transfers between devices  2.26 us (3%)
  between operations  0.74 us (1%)
    pallas_call x1, Pallas kernels, body(): pl.pallas_call(kernel, out_shape=[jax.ShapeDtypeStruct((rows, cols), f32)...  49.6 us
    ppermute x1, starting transfers between devices, body(): hi = lax.ppermute(fields[:, :HALO], 'tile', backward)  5.57 us
    ppermute x1, waiting for transfers between devices, body(): lo = lax.ppermute(fields[:, rows - HALO:], 'tile', forward)  2.25 us
    ppermute x1, starting transfers between devices, body(): lo = lax.ppermute(fields[:, rows - HALO:], 'tile', forward)  1.92 us
  transfers between devices with their start and end apart: 2, of which 1 were waited for; matrix products, arithmetic and copies ran while one was open for 6% of the time, Pallas kernels for 0%

profile of v1, /device:TPU:24, one launch (start us, length us, event | category | flops | bytes accessed | tf_op | source)
XLA Modules:
  0.0 67.1 jit_solution(16282630059072794412)
XLA Ops:
  0.6 0.0 copy-start.1
  0.6 0.0 copy-start
  0.7 1.2 %convert_bitcast_fusion = f32[1,128,1024]{2,1,0:T(8,128)S(1)} fusion(s32[128,1024]{1,0:T(8,128)} %land.1), kind=kLoop, calls=%fused_computation | loop fusion | flops 131072 | bytes 1048576 | tf_op jit(solution)/shard_map/convert_element_type | solution.py:259
  1.8 0.0 copy-done.1
  1.8 0.2 copy-done
  2.0 0.8 %pad_maximum_fusion = (f32[4,5,1024]{2,1,0:T(8,128)S(1)}, f32[4,5,1024]{2,1,0:T(8,128)S(1)}) fusion(f32[1,128,1024]{2,1,0:T(8,128)S(1)} %convert_bitcast_fusion, f32[1,128,1024]{2,1,0:T(8,128)} %param.15, f32[1,128,1024]{2,1,0:T(8,128)S(1)} %copy-done.1, f32[1,128,1024]{2,1,0:T(8,128)S(1)} %copy-done), kind=kLoop, calls=%fused_computation.2 | loop fusion | flops 122880 | bytes 2260992 | tf_op jit(solution)/shard_map/concatenate | solution.py:259
  2.8 5.6 %collective-permute-start.1 = (f32[4,5,1024]{2,1,0:T(8,128)S(1)}, f32[4,5,1024]{2,1,0:T(8,128)S(1)}, u32[]{:S(2)}, u32[]{:S(2)}) collective-permute-start(f32[4,5,1024]{2,1,0:T(8,128)S(1)} %get-tuple-element.9), channel_id=1, source_target_pairs={{1,0},{2,1},{3,2},{4,3},{5,4},{6,5},{7,6},{8,7},{9,8},{10,9},{11,1... | collective-permute-start | bytes 245768 | tf_op jit(solution)/shard_map/ppermute | solution.py:263
  8.4 1.9 %collective-permute-start = (f32[4,5,1024]{2,1,0:T(8,128)S(1)}, f32[4,5,1024]{2,1,0:T(8,128)S(1)}, u32[]{:S(2)}, u32[]{:S(2)}) collective-permute-start(f32[4,5,1024]{2,1,0:T(8,128)S(1)} %get-tuple-element.10), channel_id=1, source_target_pairs={{0,1},{1,2},{2,3},{3,4},{4,5},{5,6},{6,7},{7,8},{8,9},{9,10},{10,1... | collective-permute-start | bytes 245768 | tf_op jit(solution)/shard_map/ppermute | solution.py:262
  10.3 0.0 copy-start.5
  10.4 0.0 copy-done.7
  10.4 0.0 copy-done.8
  10.4 0.6 broadcast_in_dim_tile.7.b2
  11.0 0.7 broadcast_in_dim_tile.6.b1
  11.7 0.0 copy-done.5
  11.7 0.6 convert_bitcast_fusion.3.w1
  12.3 0.1 copy-done.6
  12.4 0.6 convert_bitcast_fusion.2.w3
  13.0 0.1 copy.17
  13.2 0.8 %convert_bitcast_fusion.1.w2 = f32[3,3,64,64]{3,2,1,0:T(8,128)} fusion(bf16[64,64,3,3]{0,1,3,2:T(8,128)(2,1)S(1)} %copy.17), kind=kLoop, calls=%fused_computation.1 | loop fusion | flops 36864 | bytes 221184 | tf_op jit(solution)/shard_map/convert_element_type | solution.py:266
  13.9 0.6 pad_add_fusion.meta
  14.5 0.0 collective-permute-done.1.hi
  14.6 2.3 %collective-permute-done.lo = f32[4,5,1024]{2,1,0:T(8,128)S(1)} collective-permute-done((f32[4,5,1024]{2,1,0:T(8,128)S(1)}, f32[4,5,1024]{2,1,0:T(8,128)S(1)}, u32[]{:S(2)}, u32[]{:S(2)}) %collective-permute-start) | collective-permute-done | bytes 81952 | tf_op jit(solution)/shard_map/ppermute | solution.py:262
  16.8 0.6 copy-done.4
  17.5 49.6 %step.1 = (f32[128,1024]{1,0:T(8,128)}, f32[128,1024]{1,0:T(8,128)}, f32[128,1024]{1,0:T(8,128)}) custom-call(s32[2]{0:T(128)} %pad_add_fusion.meta, s32[256]{0:T(256)} %depth.1, f32[3]{0:T(128)} %b3.1, f32[128,1024]{1,0:T(8,128)} %bitcast.16, f32[128,1024]{1,0:T(8,128)} %bitcast.17, f32[128,1024]{1,0:T(8,128)} %bitcast.18, s32[128,1024]{1,0:T(8,128)} %land.1, ...), custom_call_target="tpu_custom_call" | custom-call | tf_op jit(solution)/shard_map/step/pallas_call | solution.py:275
  (12 shorter events, 0.0 us)
Async XLA Ops:
  0.6 1.2 %copy-start.1 = (f32[1,128,1024]{2,1,0:T(8,128)S(1)}, f32[1,128,1024]{2,1,0:T(8,128)}, u32[]{:S(2)}) copy-start(f32[1,128,1024]{2,1,0:T(8,128)} %param.14) | copy-start | bytes 1572868
  0.6 1.4 %copy-start = (f32[1,128,1024]{2,1,0:T(8,128)S(1)}, f32[1,128,1024]{2,1,0:T(8,128)}, u32[]{:S(2)}) copy-start(f32[1,128,1024]{2,1,0:T(8,128)} %param.13) | copy-start | bytes 1572868
  2.0 8.4 %copy-start.7 = (f32[64]{0:T(128)S(1)}, f32[64]{0:T(128)}, u32[]{:S(2)}) copy-start(f32[64]{0:T(128)} %param.19) | copy-start | bytes 772
  2.0 8.4 %copy-start.8 = (f32[64]{0:T(128)S(1)}, f32[64]{0:T(128)}, u32[]{:S(2)}) copy-start(f32[64]{0:T(128)} %param.21) | copy-start | bytes 772
  2.0 11.0 %copy-start.2 = (bf16[64,64,3,3]{1,0,3,2:T(8,128)(2,1)S(1)}, bf16[64,64,3,3]{1,0,3,2:T(8,128)(2,1)}, u32[]{:S(2)}) copy-start(bf16[64,64,3,3]{1,0,3,2:T(8,128)(2,1)} %param.20) | copy-start | bytes 221188
  2.8 11.7 %collective-permute-start.1 = (f32[4,5,1024]{2,1,0:T(8,128)S(1)}, f32[4,5,1024]{2,1,0:T(8,128)S(1)}, u32[]{:S(2)}, u32[]{:S(2)}) collective-permute-start(f32[4,5,1024]{2,1,0:T(8,128)S(1)} %get-tuple-element.9), channel_id=1, source_target_pairs={{1,0},{2,1},{3,2},{4,3},{5,4},{6,5},{7,6},{8,7},{9,8},{10,9},{11,1... | collective-permute-start | bytes 245768 | tf_op jit(solution)/shard_map/ppermute | solution.py:263
  8.4 8.4 %collective-permute-start = (f32[4,5,1024]{2,1,0:T(8,128)S(1)}, f32[4,5,1024]{2,1,0:T(8,128)S(1)}, u32[]{:S(2)}, u32[]{:S(2)}) collective-permute-start(f32[4,5,1024]{2,1,0:T(8,128)S(1)} %get-tuple-element.10), channel_id=1, source_target_pairs={{0,1},{1,2},{2,3},{3,4},{4,5},{5,6},{6,7},{7,8},{8,9},{9,10},{10,1... | collective-permute-start | bytes 245768 | tf_op jit(solution)/shard_map/ppermute | solution.py:262
  10.3 1.4 %copy-start.5 = (bf16[64,3,3,3]{0,3,2,1:T(4,128)(2,1)S(1)}, bf16[64,3,3,3]{0,3,2,1:T(4,128)(2,1)}, u32[]{:S(2)}) copy-start(bf16[64,3,3,3]{0,3,2,1:T(4,128)(2,1)} %param.18) | copy-start | bytes 10372
  11.7 0.7 %copy-start.6 = (bf16[3,64,3,3]{1,3,2,0:T(4,128)(2,1)S(1)}, bf16[3,64,3,3]{1,3,2,0:T(4,128)(2,1)}, u32[]{:S(2)}) copy-start(bf16[3,64,3,3]{1,3,2,0:T(4,128)(2,1)} %param.22) | copy-start | bytes 10372
  14.5 2.3 %copy-start.3 = (f32[4,5,1024]{2,1,0:T(8,128)}, f32[4,5,1024]{2,1,0:T(8,128)S(1)}, u32[]{:S(2)}) copy-start(f32[4,5,1024]{2,1,0:T(8,128)S(1)} %collective-permute-done.1.hi) | copy-start | bytes 245764
  16.8 0.7 copy-start.4

commit v2 on v1

v2 whole, which is shorter than its diff:
```python
import jax
import jax.numpy as jnp
import numpy as np
from jax import lax
from jax.experimental import pallas as pl
from jax.experimental.pallas import tpu as pltpu
from jax.sharding import PartitionSpec as P

time_step = 0.1
viscosity = 0.5
diffusivity = 0.5
eddy_gain = 0.5
coriolis_base = 0.2
coriolis_slope = 0.6

bf16 = jnp.bfloat16
f32 = jnp.float32

TS = 128
HALO = 5
ROWS1, ROWS2, ROWS3 = 35, 34, 33
SLAB = 160
USED = 144


def select_in():
    table = np.zeros((80, 256), np.float32)
    for t in range(10):
        for s in range(8):
            table[t * 8 + s, 2 * (9 * s + t)] = 1.0
    return table


def select_out():
    table = np.zeros((2, 2, 160, 256), np.float32)
    for ip in range(2):
        for b in range(2):
            for t in range(9):
                for s in range(8):
                    place = 2 * (9 * s + t) + b
                    if place < 130:
                        table[ip, b, t * 16 + ip * 8 + s, place] = 1.0
    return table


def taps():
    for outer in range(2):
        for inner in range(2):
            for out in range(2):
                k = 2 * outer + inner - out
                if 0 <= k < 3:
                    yield outer, inner, out, k


def build_weights(w1, w2, w3, w1f, w1s, w2s, w3f, w3s):
    w1f[...] = jnp.zeros_like(w1f)
    for q in range(4):
        for dj, dy, b, ky in taps():
            for c in range(3):
                for a in range(2):
                    row = dj * 128 + dy * 48 + c * 16 + 4 + 2 * q + a
                    lane = (a * 2 + b) * 64
                    w1f[q, row : row + 3, lane : lane + 64] = 0.5 * w1[c, ky]
    w1s[...] = w1f[...].astype(bf16)
    w2s[...] = jnp.zeros_like(w2s)
    for di, ai, ao, kx in taps():
        for dj, bi, bo, ky in taps():
            row = (ai * 2 + bi) * 64
            lane = (ao * 2 + bo) * 64
            w2s[di * 2 + dj, row : row + 64, lane : lane + 64] = (0.5 * w2[kx, ky]).astype(bf16)
    w3f[...] = jnp.zeros_like(w3f)
    for di, ai, ao, kx in taps():
        for dj, bi, bo, ky in taps():
            lane = (ai * 2 + bi) * 64
            for c in range(3):
                row = (di * 2 + dj) * 16 + bo * 6 + c * 2 + ao
                w3f[row : row + 1, lane : lane + 64] = w3[c, kx, ky : ky + 1]
    w3s[...] = w3f[...].astype(bf16)


def wet_line(depth, level, tile_row, lane, across):
    line = jnp.zeros(lane.shape, f32)
    for ty in range(across):
        wet = (depth[tile_row * across + ty] > level).astype(f32)
        line = jnp.where(lane // TS == ty, wet, line)
    return line


def feature_rows(k, tile, rows_all, wet, ext, landx, east, north, tracer, feat, act, act0, store):
    cols = landx.shape[1]
    lane = lax.broadcasted_iota(jnp.int32, (8, cols), 1)
    row = lax.broadcasted_iota(jnp.int32, (8, cols), 0)
    zeros = jnp.zeros((8, TS), f32)

    def west(x):
        return jnp.where(lane == 0, 0.0, pltpu.roll(x, 1, 1))

    def east_of(x):
        return jnp.where(lane == cols - 1, 0.0, pltpu.roll(x, cols - 1, 1))

    base = 8 * k + 16
    if not isinstance(k, int):
        base = pl.multiple_of(base, 8)
    water = jnp.where(landx[pl.ds(base, 8), :] == 1, 1.0, 0.0)
    active = water * wet
    above = base - 8 if isinstance(k, int) else pl.multiple_of(base - 8, 8)
    around = [ext[f, pl.ds(above, 24), :] for f in range(3)]
    mid = [x[8:16] for x in around]
    up = [x[7:15] for x in around]
    down = [x[9:17] for x in around]
    left = [west(x) for x in mid]
    right = [east_of(x) for x in mid]
    lap = [down[f] + up[f] + right[f] + left[f] - 4.0 * mid[f] for f in range(3)]
    grad_east = 0.5 * (down[2] - up[2])
    grad_north = 0.5 * (right[2] - left[2])
    place = (tile * TS + 8 * k + row).astype(f32)
    coriolis = coriolis_base + coriolis_slope * (place + 0.5) / rows_all
    step = time_step * active
    new_east = mid[0] + step * (coriolis * mid[1] - grad_east + viscosity * lap[0])
    new_north = mid[1] + step * (-coriolis * mid[0] - grad_north + viscosity * lap[1])
    new_tracer = mid[2] + step * (
        -(mid[0] * grad_east + mid[1] * grad_north) + diffusivity * lap[2]
    )
    if store:
        at = 8 * k
        if not isinstance(k, int):
            at = pl.multiple_of(at, 8)
        east[pl.ds(at, 8), :] = new_east
        north[pl.ds(at, 8), :] = new_north
        tracer[pl.ds(at, 8), :] = new_tracer
    q = 8 * k + 8
    if not isinstance(k, int):
        q = pl.multiple_of(q, 8)
    for c, new in enumerate((new_east, new_north, new_tracer)):
        wide = jnp.concatenate([new * active, zeros], axis=1)
        feat[c, pl.ds(q, 8), :] = pltpu.roll(wide, 4, 1)
    act[pl.ds(q, 8), :] = pltpu.roll(jnp.concatenate([active, zeros], axis=1), 1, 1)
    act0[pl.ds(q, 8), :] = pltpu.roll(jnp.concatenate([water, zeros], axis=1), 1, 1)


def silu_half(half):
    return half + half * jnp.tanh(half)


def store_slab(ref, index, value):
    ref[index, 0:USED, :] = value.astype(bf16)
    ref[index, USED:SLAB, :] = pltpu.roll(value[0:16], 15, 0).astype(bf16)


def closure_tile(win, mwin, res, sel_in, sel_out, b1, b2, b3, w1s, w2s, w3s, patches, h1, h2, parts, flat):
    for g in range(9):
        halves = []
        for ip in range(2):
            base = 64 * ip + 8 * g
            rows = win[:, base : base + 16, :].reshape(48, 256)
            rows = jnp.concatenate([rows, pltpu.roll(rows, 255, 1), jnp.zeros((32, 256), f32)], axis=0)
            got = lax.dot_general(
                sel_in[...], rows.astype(bf16), (((1,), (1,)), ((), ())), preferred_element_type=f32
            )
            halves.append(got.reshape(10, 8, 128))
        patches[g] = jnp.stack(halves, axis=1).reshape(SLAB, 128).astype(bf16)
    for q in range(4):
        for g in range(9):
            if 4 * g + q >= ROWS1:
                continue
            lhs = jnp.concatenate([patches[g, 0:USED, :], patches[g, 16:SLAB, :]], axis=1)
            half = jnp.dot(lhs, w1s[q], preferred_element_type=f32) + b1[...]
            store_slab(h1, 4 * g + q, silu_half(half))
    for i in range(0, ROWS2, 2):
        half = b2[...]
        for di in range(2):
            for dj in range(2):
                lhs = h1[i + di : i + di + 2, 16 * dj : 16 * dj + USED, :].reshape(2 * USED, 256)
                half = half + jnp.dot(lhs, w2s[2 * di + dj], preferred_element_type=f32)
        out = silu_half(half)
        store_slab(h2, i, out[0:USED])
        store_slab(h2, i + 1, out[USED:])
    for i in range(ROWS2):
        parts[i] = lax.dot_general(
            w3s[...], h2[i], (((1,), (1,)), ((), ())), preferred_element_type=f32
        )
    for i in range(ROWS3):
        got = (
            parts[i, 0:16, 0:USED]
            + parts[i, 16:32, 16:SLAB]
            + parts[i + 1, 32:48, 0:USED]
            + parts[i + 1, 48:64, 16:SLAB]
        )
        for b in range(2):
            for c in range(3):
                r = b * 6 + c * 2
                flat[b, c, 2 * i : 2 * i + 2, 0:USED] = got[r : r + 2] + b3[c]
    for ip in range(2):
        mask = mwin[8 + 64 * ip - 1 : 8 + 64 * ip + 65, :]
        masked = []
        for c in range(3):
            image = jnp.zeros((72, 256), f32)
            for b in range(2):
                image = image + jnp.dot(
                    flat[b, c].astype(bf16), sel_out[ip, b], preferred_element_type=f32
                )
            masked.append(image[0:66] * mask)
        xx, xy, yy = masked

        def dx(m):
            return 0.5 * (m[2:66, 1:129] - m[0:64, 1:129])

        def dy(m):
            return 0.5 * (m[1:65, 2:130] - m[1:65, 0:128])

        gain = eddy_gain * mask[1:65, 1:129]
        rows = slice(64 * ip, 64 * ip + 64)
        res[0, rows, :] = gain * (dx(xx) + dy(xy))
        res[1, rows, :] = gain * (dx(xy) + dy(yy))


def add_push(east, north, res, lane0):
    east[:, pl.ds(lane0, TS)] += res[0]
    north[:, pl.ds(lane0, TS)] += res[1]


KEPT = 5


def first_kernel(
    depth, b3, u, v, t, land, w1, b1, w2, b2, w3, sel_in, sel_out, pick,
    east, north, tracer, feat_out, act_out, w1s, w2s, w3s,
    ext, landx, feat, act, act0, w1f, w3f, patches, h1, h2, parts, flat, win, mwin, res,
    main_out, edge_out, main_in, edge_in, res_out, res_in,
    halo_send, halo_recv, win_send, win_recv, res_send, res_recv,
):
    level, tile = lax.axis_index("group"), lax.axis_index("tile")
    tiles = lax.axis_size("tile")
    cols = u.shape[1]
    across = cols // TS
    mesh_id = pl.DeviceIdType.MESH

    barrier = pltpu.get_barrier_semaphore()

    def greet(group, place):
        pl.semaphore_signal(barrier, inc=1, device_id=(group, place), device_id_type=mesh_id)

    @pl.when(tile > 0)
    def _():
        greet(level, tile - 1)

    @pl.when(tile < tiles - 1)
    def _():
        greet(level, tile + 1)

    @pl.when(level == 0)
    def _():
        greet(2, tile)
        greet(3, tile)

    @pl.when(level >= 2)
    def _():
        greet(0, tile)

    peers = jnp.where(tile > 0, 1, 0) + jnp.where(tile < tiles - 1, 1, 0)
    peers = peers + jnp.where(level == 0, 2, jnp.where(level == 1, 0, 1))
    pl.semaphore_wait(barrier, peers)

    def halo_copy(way, f):
        src = (u, v, t, land)[f]
        rows_from, rows_to, place = ((TS - 8, 8, tile + 1), (0, 144, tile - 1))[way]
        dst = ext.at[f, pl.ds(rows_to, 8)] if f < 3 else landx.at[pl.ds(rows_to, 8)]
        return pltpu.make_async_remote_copy(
            src_ref=src.at[pl.ds(rows_from, 8)],
            dst_ref=dst,
            send_sem=halo_send.at[way, f],
            recv_sem=halo_recv.at[way, f],
            device_id=(level, place),
            device_id_type=mesh_id,
        )

    @pl.when(tile < tiles - 1)
    def _():
        for f in range(4):
            halo_copy(0, f).start()

    @pl.when(tile > 0)
    def _():
        for f in range(4):
            halo_copy(1, f).start()

    for f, src in enumerate((u, v, t)):
        ext[f, 0:8, :] = jnp.zeros((8, cols), f32)
        ext[f, 152:160, :] = jnp.zeros((8, cols), f32)
        ext[f, 16:144, :] = src[...]
    landx[0:8, :] = jnp.zeros((8, cols), jnp.int32)
    landx[152:160, :] = jnp.zeros((8, cols), jnp.int32)
    landx[16:144, :] = land[...]

    @pl.when(tile == 0)
    def _():
        for f in range(3):
            ext[f, 8:16, :] = jnp.zeros((8, cols), f32)
        landx[8:16, :] = jnp.zeros((8, cols), jnp.int32)

    @pl.when(tile == tiles - 1)
    def _():
        for f in range(3):
            ext[f, 144:152, :] = jnp.zeros((8, cols), f32)
        landx[144:152, :] = jnp.zeros((8, cols), jnp.int32)

    lane = lax.broadcasted_iota(jnp.int32, (8, cols), 1)
    rows_all = float(tiles * TS)
    wet_mid = wet_line(depth, level, tile, lane, across)
    wet_low = wet_line(depth, level, (tile + tiles - 1) % tiles, lane, across)
    wet_high = wet_line(depth, level, (tile + 1) % tiles, lane, across)

    def rows_of(k, wet, store):
        feature_rows(
            k, tile, rows_all, wet, ext, landx, east, north, tracer, feat, act, act0, store
        )

    def inner(k, carry):
        rows_of(k, wet_mid, True)
        return carry

    lax.fori_loop(1, 15, inner, 0)

    @pl.when(tile > 0)
    def _():
        for f in range(4):
            halo_copy(0, f).wait_recv()

    @pl.when(tile < tiles - 1)
    def _():
        for f in range(4):
            halo_copy(1, f).wait_recv()

    rows_of(-1, wet_low, False)
    rows_of(0, wet_mid, True)
    rows_of(15, wet_mid, True)
    rows_of(16, wet_high, False)

    def window_copy(slot, part):
        group, place = ((2, 0), (3, 0), (3, 1))[slot]
        src, dst = ((main_out, main_in), (edge_out, edge_in))[part]
        return pltpu.make_async_remote_copy(
            src_ref=src.at[slot],
            dst_ref=dst.at[place],
            send_sem=win_send.at[slot, part],
            recv_sem=win_recv.at[place, part],
            device_id=(group, tile),
            device_id_type=mesh_id,
        )

    @pl.when(level == 0)
    def _():
        for slot in (1, 0, 2):
            lane0 = (KEPT + slot) * TS
            main_out[slot] = feat[:, :, lane0 : lane0 + TS].astype(bf16)
            edge = feat[:, :, lane0 + TS : lane0 + 2 * TS].reshape(432, TS).astype(bf16)
            edge_out[slot] = lax.dot_general(
                pick[...], edge, (((1,), (1,)), ((), ())), preferred_element_type=f32
            ).astype(bf16)
            for part in range(2):
                window_copy(slot, part).start()

    build_weights(w1, w2, w3, w1f, w1s, w2s, w3f, w3s)
    flat[...] = jnp.zeros_like(flat)
    feat_out[...] = feat[...].astype(bf16)
    act_out[...] = act[...]

    def result_copy(item):
        return pltpu.make_async_remote_copy(
            src_ref=res_out.at[item],
            dst_ref=res_in.at[level - 2 + item],
            send_sem=res_send.at[item],
            recv_sem=res_recv.at[level - 2 + item],
            device_id=(0, tile),
            device_id_type=mesh_id,
        )

    def item_step(item, carry):
        lane0 = pl.multiple_of(item * TS, TS)

        @pl.when(level == 0)
        def _():
            win[...] = feat[:, :, pl.ds(lane0, 2 * TS)]
            mwin[...] = act[:, pl.ds(lane0, 2 * TS)]

        @pl.when(level >= 2)
        def _():
            for part in range(2):
                src, dst = ((main_out, main_in), (edge_out, edge_in))[part]
                pltpu.make_async_remote_copy(
                    src_ref=src.at[0],
                    dst_ref=dst.at[item],
                    send_sem=win_send.at[0, part],
                    recv_sem=win_recv.at[item, part],
                    device_id=(0, tile),
                    device_id_type=mesh_id,
                ).wait_recv()
            win[:, :, 0:TS] = main_in[item].astype(f32)
            edge = lax.dot_general(
                edge_in[item], pick[...], (((0,), (0,)), ((), ())), preferred_element_type=f32
            )
            win[:, :, TS : 2 * TS] = edge.reshape(3, 144, TS)
            from0 = pl.multiple_of((KEPT + level - 2 + item) * TS, TS)
            mwin[...] = act0[:, pl.ds(from0, 2 * TS)]

        closure_tile(
            win, mwin, res, sel_in, sel_out, b1, b2, b3, w1s, w2s, w3s, patches, h1, h2, parts, flat
        )

        @pl.when(level == 0)
        def _():
            add_push(east, north, res, lane0)

        @pl.when(level >= 2)
        def _():
            res_out[item] = res[...]
            result_copy(item).start()

        return carry

    here = jnp.where(level == 0, KEPT, jnp.where(level == 1, 0, level - 1))
    lax.fori_loop(0, here, item_step, 0)

    @pl.when(level == 0)
    def _():
        for slot in range(3):
            pltpu.make_async_remote_copy(
                src_ref=res_out.at[0],
                dst_ref=res_in.at[slot],
                send_sem=res_send.at[0],
                recv_sem=res_recv.at[slot],
                device_id=(3, tile),
                device_id_type=mesh_id,
            ).wait_recv()
            lane0 = (KEPT + slot) * TS
            east[:, lane0 : lane0 + TS] += res_in[slot, 0]
            north[:, lane0 : lane0 + TS] += res_in[slot, 1]
            for part in range(2):
                window_copy(slot, part).wait_send()

    @pl.when(level == 2)
    def _():
        result_copy(0).wait_send()

    @pl.when(level == 3)
    def _():
        result_copy(0).wait_send()
        result_copy(1).wait_send()

    @pl.when(tile < tiles - 1)
    def _():
        for f in range(4):
            halo_copy(0, f).wait_send()

    @pl.when(tile > 0)
    def _():
        for f in range(4):
            halo_copy(1, f).wait_send()


def second_kernel(
    depth, meta, b3, east1, north1, feat, act, w1s, w2s, w3s, b1, b2, sel_in, sel_out,
    east, north,
    patches, h1, h2, parts, flat, win, mwin, res,
):
    level, tile = meta[0], meta[1]
    across = east.shape[1] // TS
    east[...] = east1[...]
    north[...] = north1[...]

    @pl.when(level > 0)
    def _():
        flat[...] = jnp.zeros_like(flat)

        def column(ty, carry):
            @pl.when(depth[tile * across + ty] > level)
            def _():
                lane0 = pl.multiple_of(ty * TS, TS)
                win[...] = feat[:, :, pl.ds(lane0, 2 * TS)].astype(f32)
                mwin[...] = act[:, pl.ds(lane0, 2 * TS)]
                closure_tile(
                    win, mwin, res, sel_in, sel_out, b1, b2, b3, w1s, w2s, w3s,
                    patches, h1, h2, parts, flat,
                )
                add_push(east, north, res, lane0)

            return carry

        lax.fori_loop(0, across, column, 0)


def body(u, v, t, land, depth, conv_one, bias_one, conv_two, bias_two, conv_three, bias_three):
    levels, rows, cols = u.shape
    w1 = conv_one.transpose(1, 3, 2, 0).astype(f32)
    w2 = conv_two.transpose(2, 3, 1, 0).astype(f32)
    w3 = conv_three.transpose(0, 2, 3, 1).astype(f32)
    b1 = jnp.tile(0.5 * bias_one, 4)[None]
    b2 = jnp.tile(0.5 * bias_two, 4)[None]
    sel_in = jnp.asarray(select_in(), bf16)
    sel_out = jnp.asarray(select_out(), bf16)
    pick = jnp.asarray(np.eye(16, TS, dtype=np.float32), bf16)
    meta = jnp.stack([lax.axis_index("group"), lax.axis_index("tile")]).astype(jnp.int32)
    vmem = pl.BlockSpec(memory_space=pltpu.VMEM)
    smem = pl.BlockSpec(memory_space=pltpu.SMEM)
    wide = cols + TS
    plane = jax.ShapeDtypeStruct((rows, cols), f32)
    work = [
        pltpu.VMEM((9, SLAB, TS), bf16),
        pltpu.VMEM((ROWS1 + 1, SLAB, 256), bf16),
        pltpu.VMEM((ROWS2, SLAB, 256), bf16),
        pltpu.VMEM((ROWS2, 64, SLAB), f32),
        pltpu.VMEM((2, 3, 72, SLAB), f32),
        pltpu.VMEM((3, 144, 2 * TS), f32),
        pltpu.VMEM((144, 2 * TS), f32),
        pltpu.VMEM((2, TS, TS), f32),
    ]
    east1, north1, tracer, feat, act, w1s, w2s, w3s = pl.pallas_call(
        first_kernel,
        out_shape=[plane] * 3
        + [
            jax.ShapeDtypeStruct((3, 144, wide), bf16),
            jax.ShapeDtypeStruct((144, wide), f32),
            jax.ShapeDtypeStruct((4, 256, 256), bf16),
            jax.ShapeDtypeStruct((4, 256, 256), bf16),
            jax.ShapeDtypeStruct((64, 256), bf16),
        ],
        in_specs=[smem] * 2 + [vmem] * 12,
        out_specs=[vmem] * 8,
        scratch_shapes=[
            pltpu.VMEM((3, 160, cols), f32),
            pltpu.VMEM((160, cols), jnp.int32),
            pltpu.VMEM((3, 144, wide), f32),
            pltpu.VMEM((144, wide), f32),
            pltpu.VMEM((144, wide), f32),
            pltpu.VMEM((4, 256, 256), f32),
            pltpu.VMEM((64, 256), f32),
        ]
        + work
        + [
            pltpu.VMEM((3, 3, 144, TS), bf16),
            pltpu.VMEM((3, 16, 432), bf16),
            pltpu.VMEM((2, 3, 144, TS), bf16),
            pltpu.VMEM((2, 16, 432), bf16),
            pltpu.VMEM((2, 2, TS, TS), f32),
            pltpu.VMEM((3, 2, TS, TS), f32),
            pltpu.SemaphoreType.DMA((2, 4)),
            pltpu.SemaphoreType.DMA((2, 4)),
            pltpu.SemaphoreType.DMA((3, 2)),
            pltpu.SemaphoreType.DMA((2, 2)),
            pltpu.SemaphoreType.DMA((2,)),
            pltpu.SemaphoreType.DMA((3,)),
        ],
        compiler_params=pltpu.CompilerParams(
            vmem_limit_bytes=40 * 2**20, collective_id=0, has_side_effects=True
        ),
        name="first",
    )(depth, bias_three, u[0], v[0], t[0], land, w1, b1, w2, b2, w3, sel_in, sel_out, pick)
    east, north = pl.pallas_call(
        second_kernel,
        out_shape=[plane] * 2,
        in_specs=[smem] * 3 + [vmem] * 11,
        out_specs=[vmem] * 2,
        scratch_shapes=work,
        compiler_params=pltpu.CompilerParams(vmem_limit_bytes=40 * 2**20),
        name="second",
    )(depth, meta, bias_three, east1, north1, feat, act, w1s, w2s, w3s, b1, b2, sel_in, sel_out)
    return east[None], north[None], tracer[None]


def solution(mesh):
    field = P("group", "tile", None)
    in_specs = (field, field, field, P("tile", None)) + (P(),) * 7
    return jax.shard_map(
        body, mesh=mesh, in_specs=in_specs, out_specs=(field,) * 3, check_vma=False
    )
```

time: 67.4 us -> 51.9 us (0.77)
  starting transfers between devices: 7.49 us -> 0 us
  Pallas kernels: 49.6 us -> 42.3 us
  local copies, waits for them, and re-layouts: 2.38 us -> 8.31 us
  other arithmetic: 4.6 us -> 0.11 us
  waiting for transfers between devices: 2.26 us -> 0 us
    ppermute x2 -> x0, starting transfers between devices: 7.49 us -> none  [the longest x1 5.57 us: body(): hi = lax.ppermute(fields[:, :HALO], 'tile', backward)]
    pallas_call x1 -> x2, Pallas kernels: 49.6 us -> 42.3 us  [the longest x1 40.5 us: body(): pl.pallas_call(first_kernel, out_shape=[plane] * 3 + [jax.ShapeDtypeStruc...]
    unnamed x19 -> x28, local copies, waits for them, and re-layouts: 1.09 us -> 8.14 us
    ppermute x2 -> x0, waiting for transfers between devices: 2.26 us -> none  [the longest x1 2.25 us: body(): lo = lax.ppermute(fields[:, rows - HALO:], 'tile', forward)]
    convert_element_type x1 -> x0, other arithmetic: 1.16 us -> none  [body(): fields = jnp.concatenate([u, v, t, land[None].astype(f32)], axis=0)]
    concatenate x1 -> x0, other arithmetic: 0.84 us -> none  [body(): fields = jnp.concatenate([u, v, t, land[None].astype(f32)], axis=0)]
    convert_element_type x1, other arithmetic: 0.75 us -> 0.02 us  [body(): w2 = conv_two.transpose(2, 3, 1, 0).astype(f32)]
  transfers between devices with their start and end apart: 2 -> 0, of which waited for: 1 -> 0; matrix products, arithmetic and copies ran while one was open for 6% -> 0% of each run, Pallas kernels for 0% -> 0%
where the time goes in v2:
time: 51.9 us; the launch traced here: 51.4 us
  Pallas kernels  42.3 us (82%)
  local copies, waits for them, and re-layouts  8.31 us (16%)
  between operations  0.72 us (1%)
    pallas_call x1, Pallas kernels, body(): pl.pallas_call(first_kernel, out_shape=[plane] * 3 + [jax.ShapeDtypeStruc...  40.5 us
    unnamed x28, local copies, waits for them, and re-layouts  8.14 us
    pallas_call x1, Pallas kernels, body(): pl.pallas_call(second_kernel, out_shape=[plane] * 2, in_specs=[smem] * 3...  1.78 us

profile of v2, /device:TPU:24, one launch (start us, length us, event | category | flops | bytes accessed | tf_op | source)
XLA Modules:
  0.0 51.4 jit_solution(1942253495983008707)
XLA Ops:
  0.6 0.1 pad_add_fusion.meta
  0.7 0.6 %copy-done.11 = f32[64]{0:T(128)S(1)} copy-done((f32[64]{0:T(128)S(1)}, f32[64]{0:T(128)}, u32[]{:S(2)}) %copy-start.11) | copy-done | bytes 280
  1.4 0.0 copy-done.12
  1.4 0.1 broadcast_in_dim_tile.7.b2
  1.5 0.1 broadcast_in_dim_tile.6.b1
  1.6 0.0 copy-done.9
  1.6 0.7 %copy-done.10 = bf16[3,64,3,3]{1,3,2,0:T(4,128)(2,1)S(1)} copy-done((bf16[3,64,3,3]{1,3,2,0:T(4,128)(2,1)S(1)}, bf16[3,64,3,3]{1,3,2,0:T(4,128)(2,1)}, u32[]{:S(2)}) %copy-start.10) | copy-done | bytes 3480
  2.3 1.1 %copy.18 = bf16[64,64,3,3]{0,1,3,2:T(8,128)(2,1)S(1)} copy(bf16[64,64,3,3]{1,0,3,2:T(8,128)(2,1)} %param.21) | data formatting | bytes 147456 | tf_op args[7]
  3.4 0.0 copy-start.5
  3.4 0.0 copy-start.6
  3.4 0.0 copy-start.7
  3.4 0.0 copy-start.8
  3.5 0.0 copy-done
  3.5 0.7 %copy-done.5 = bf16[80,256]{1,0:T(8,128)(2,1)S(1)} copy-done((bf16[80,256]{1,0:T(8,128)(2,1)S(1)}, bf16[80,256]{1,0:T(8,128)(2,1)}, u32[]{:S(2)}) %copy-start.5) | copy-done | bytes 40984
  4.2 0.0 copy-done.6
  4.2 0.0 copy-done.7
  4.2 0.0 copy-done.8
  4.2 1.0 %copy-done.1 = f32[1,128,1024]{2,1,0:T(8,128)S(1)} copy-done((f32[1,128,1024]{2,1,0:T(8,128)S(1)}, f32[1,128,1024]{2,1,0:T(8,128)}, u32[]{:S(2)}) %copy-start.1) | copy-done | bytes 524312
  5.2 1.0 %copy-done.2 = f32[1,128,1024]{2,1,0:T(8,128)S(1)} copy-done((f32[1,128,1024]{2,1,0:T(8,128)S(1)}, f32[1,128,1024]{2,1,0:T(8,128)}, u32[]{:S(2)}) %copy-start.2) | copy-done | bytes 524312
  6.3 1.0 %copy-done.3 = f32[1,128,1024]{2,1,0:T(8,128)S(1)} copy-done((f32[1,128,1024]{2,1,0:T(8,128)S(1)}, f32[1,128,1024]{2,1,0:T(8,128)}, u32[]{:S(2)}) %copy-start.3) | copy-done | bytes 524312
  7.3 1.0 %copy-done.4 = s32[128,1024]{1,0:T(8,128)S(1)} copy-done((s32[128,1024]{1,0:T(8,128)S(1)}, s32[128,1024]{1,0:T(8,128)}, u32[]{:S(2)}) %copy-start.4) | copy-done | bytes 524312
  8.3 40.5 %first.1 = (f32[128,1024]{1,0:T(8,128)S(1)}, f32[128,1024]{1,0:T(8,128)S(1)}, f32[128,1024]{1,0:T(8,128)S(1)}, bf16[3,144,1152]{2,1,0:T(8,128)(2,1)S(1)}, f32[14...) custom-call(s32[256]{0:T(256)S(1)} %copy-done.7, ...), custom_call_target="tpu_custom_call" | custom-call | tf_op jit(solution)/shard_map/first/pallas_call | solution.py:517
  48.9 1.8 %second.1 = (f32[128,1024]{1,0:T(8,128)}, f32[128,1024]{1,0:T(8,128)}) custom-call(s32[256]{0:T(256)S(1)} %copy-done.7, s32[2]{0:T(128)S(1)} %pad_add_fusion.meta, f32[3]{0:T(128)S(1)} %copy-done.8, f32[128,1024]{1,0:T(8,128)S(1)} %get-tuple-element.13.east1, f32[128,1024]{1,0:T(8,128)S(1)} %get-tuple-element.14.north1, ...), custom_call_target="tpu_custom_call" | custom-call | tf_op jit(solution)/shard_map/second/pallas_call | solution.py:558
  50.6 0.8 %copy.21 = f32[1,128,1024]{2,1,0:T(8,128)} copy(f32[1,128,1024]{2,1,0:T(8,128)S(1)} %bitcast.17) | data formatting | bytes 1048576
  (16 shorter events, 0.1 us)
Async XLA Ops:
  0.7 0.7 %copy-start.11 = (f32[64]{0:T(128)S(1)}, f32[64]{0:T(128)}, u32[]{:S(2)}) copy-start(f32[64]{0:T(128)} %param.20) | copy-start | bytes 772
  0.7 0.7 %copy-start.12 = (f32[64]{0:T(128)S(1)}, f32[64]{0:T(128)}, u32[]{:S(2)}) copy-start(f32[64]{0:T(128)} %param.22) | copy-start | bytes 772
  0.7 0.9 %copy-start.9 = (bf16[64,3,3,3]{0,3,2,1:T(4,128)(2,1)S(1)}, bf16[64,3,3,3]{0,3,2,1:T(4,128)(2,1)}, u32[]{:S(2)}) copy-start(bf16[64,3,3,3]{0,3,2,1:T(4,128)(2,1)} %param.19) | copy-start | bytes 10372
  1.6 0.7 %copy-start.10 = (bf16[3,64,3,3]{1,3,2,0:T(4,128)(2,1)S(1)}, bf16[3,64,3,3]{1,3,2,0:T(4,128)(2,1)}, u32[]{:S(2)}) copy-start(bf16[3,64,3,3]{1,3,2,0:T(4,128)(2,1)} %param.23) | copy-start | bytes 10372
  2.3 1.2 %copy-start = (bf16[2,2,160,256]{3,2,1,0:T(8,128)(2,1)S(1)}, bf16[2,2,160,256]{3,2,1,0:T(8,128)(2,1)}, u32[]{:S(2)}) copy-start(bf16[2,2,160,256]{3,2,1,0:T(8,128)(2,1)} %constant.18.clone.sel_out) | copy-start | bytes 983044
  3.4 0.8 %copy-start.5 = (bf16[80,256]{1,0:T(8,128)(2,1)S(1)}, bf16[80,256]{1,0:T(8,128)(2,1)}, u32[]{:S(2)}) copy-start(bf16[80,256]{1,0:T(8,128)(2,1)} %constant.17.clone.sel_in) | copy-start | bytes 122884
  3.4 0.8 %copy-start.6 = (bf16[16,128]{1,0:T(8,128)(2,1)S(1)}, bf16[16,128]{1,0:T(8,128)(2,1)}, u32[]{:S(2)}) copy-start(bf16[16,128]{1,0:T(8,128)(2,1)} %constant.19.clone.pick) | copy-start | bytes 12292
  3.4 0.8 %copy-start.7 = (s32[256]{0:T(256)S(1)}, s32[256]{0:T(256)}, u32[]{:S(2)}) copy-start(s32[256]{0:T(256)} %depth.3) | copy-start | bytes 3076
  3.4 0.8 %copy-start.8 = (f32[3]{0:T(128)S(1)}, f32[3]{0:T(128)}, u32[]{:S(2)}) copy-start(f32[3]{0:T(128)} %b3.3) | copy-start | bytes 40
  4.2 1.0 %copy-start.1 = (f32[1,128,1024]{2,1,0:T(8,128)S(1)}, f32[1,128,1024]{2,1,0:T(8,128)}, u32[]{:S(2)}) copy-start(f32[1,128,1024]{2,1,0:T(8,128)} %param.14) | copy-start | bytes 1572868
  5.2 1.0 %copy-start.2 = (f32[1,128,1024]{2,1,0:T(8,128)S(1)}, f32[1,128,1024]{2,1,0:T(8,128)}, u32[]{:S(2)}) copy-start(f32[1,128,1024]{2,1,0:T(8,128)} %param.15) | copy-start | bytes 1572868
  6.3 1.0 %copy-start.3 = (f32[1,128,1024]{2,1,0:T(8,128)S(1)}, f32[1,128,1024]{2,1,0:T(8,128)}, u32[]{:S(2)}) copy-start(f32[1,128,1024]{2,1,0:T(8,128)} %param.16) | copy-start | bytes 1572868
  7.3 1.0 %copy-start.4 = (s32[128,1024]{1,0:T(8,128)S(1)}, s32[128,1024]{1,0:T(8,128)}, u32[]{:S(2)}) copy-start(s32[128,1024]{1,0:T(8,128)} %land.1) | copy-start | bytes 1572868

commit v3 on v2

--- a/solution.py
+++ b/solution.py
@@ -1,6 +1,5 @@
 import jax
 import jax.numpy as jnp
-import numpy as np
 from jax import lax
 from jax.experimental import pallas as pl
 from jax.experimental.pallas import tpu as pltpu
@@ -23,24 +22,21 @@
 USED = 144
 
 
-def select_in():
-    table = np.zeros((80, 256), np.float32)
-    for t in range(10):
-        for s in range(8):
-            table[t * 8 + s, 2 * (9 * s + t)] = 1.0
-    return table
-
-
-def select_out():
-    table = np.zeros((2, 2, 160, 256), np.float32)
+def build_tables(sel_in, sel_out, pick):
+    row = lax.broadcasted_iota(jnp.int32, (80, 256), 0)
+    col = lax.broadcasted_iota(jnp.int32, (80, 256), 1)
+    sel_in[...] = (col == 2 * (9 * (row % 8) + row // 8)).astype(f32).astype(bf16)
+    row = lax.broadcasted_iota(jnp.int32, (160, 256), 0)
+    col = lax.broadcasted_iota(jnp.int32, (160, 256), 1)
+    place = 2 * (9 * (row % 8) + row // 16)
+    inside = (row < USED) & (col < 130)
     for ip in range(2):
         for b in range(2):
-            for t in range(9):
-                for s in range(8):
-                    place = 2 * (9 * s + t) + b
-                    if place < 130:
-                        table[ip, b, t * 16 + ip * 8 + s, place] = 1.0
-    return table
+            hit = inside & ((row % 16) // 8 == ip) & (col == place + b)
+            sel_out[ip, b] = hit.astype(f32).astype(bf16)
+    row = lax.broadcasted_iota(jnp.int32, (16, TS), 0)
+    col = lax.broadcasted_iota(jnp.int32, (16, TS), 1)
+    pick[...] = (row == col).astype(f32).astype(bf16)
 
 
 def taps():
@@ -52,30 +48,43 @@
                     yield outer, inner, out, k
 
 
-def build_weights(w1, w2, w3, w1f, w1s, w2s, w3f, w3s):
+def build_weights(w1, w2, w3, b1, b2, w1f, w1s, w2s, w3f, w3s, b1r, b2r):
     w1f[...] = jnp.zeros_like(w1f)
-    for q in range(4):
-        for dj, dy, b, ky in taps():
-            for c in range(3):
-                for a in range(2):
-                    row = dj * 128 + dy * 48 + c * 16 + 4 + 2 * q + a
-                    lane = (a * 2 + b) * 64
-                    w1f[q, row : row + 3, lane : lane + 64] = 0.5 * w1[c, ky]
+    for c in range(3):
+        for kx in range(3):
+            line = 0.5 * w1[c, kx].astype(f32)
+            for q in range(4):
+                for dj, dy, b, ky in taps():
+                    for a in range(2):
+                        row = dj * 128 + dy * 48 + c * 16 + 4 + 2 * q + a + kx
+                        lane = (a * 2 + b) * 64
+                        w1f[q, row : row + 1, lane : lane + 64] = line[ky : ky + 1]
     w1s[...] = w1f[...].astype(bf16)
     w2s[...] = jnp.zeros_like(w2s)
-    for di, ai, ao, kx in taps():
-        for dj, bi, bo, ky in taps():
-            row = (ai * 2 + bi) * 64
-            lane = (ao * 2 + bo) * 64
-            w2s[di * 2 + dj, row : row + 64, lane : lane + 64] = (0.5 * w2[kx, ky]).astype(bf16)
+    for kx in range(3):
+        for ky in range(3):
+            block = (0.5 * w2[kx, ky].astype(f32)).T.astype(bf16)
+            for di, ai, ao, kx_here in taps():
+                for dj, bi, bo, ky_here in taps():
+                    if (kx, ky) == (kx_here, ky_here):
+                        row = (ai * 2 + bi) * 64
+                        lane = (ao * 2 + bo) * 64
+                        w2s[di * 2 + dj, row : row + 64, lane : lane + 64] = block
     w3f[...] = jnp.zeros_like(w3f)
-    for di, ai, ao, kx in taps():
-        for dj, bi, bo, ky in taps():
-            lane = (ai * 2 + bi) * 64
-            for c in range(3):
-                row = (di * 2 + dj) * 16 + bo * 6 + c * 2 + ao
-                w3f[row : row + 1, lane : lane + 64] = w3[c, kx, ky : ky + 1]
+    for c in range(3):
+        for kx in range(3):
+            line = w3[c, kx].astype(f32)
+            for di, ai, ao, kx_here in taps():
+                if kx != kx_here:
+                    continue
+                for dj, bi, bo, ky in taps():
+                    lane = (ai * 2 + bi) * 64
+                    row = (di * 2 + dj) * 16 + bo * 6 + c * 2 + ao
+                    w3f[row : row + 1, lane : lane + 64] = line[ky : ky + 1]
     w3s[...] = w3f[...].astype(bf16)
+    for j in range(4):
+        b1r[:, 64 * j : 64 * j + 64] = 0.5 * b1[...]
+        b2r[:, 64 * j : 64 * j + 64] = 0.5 * b2[...]
 
 
 def wet_line(depth, level, tile_row, lane, across):
@@ -223,11 +232,12 @@
 
 
 def first_kernel(
-    depth, b3, u, v, t, land, w1, b1, w2, b2, w3, sel_in, sel_out, pick,
-    east, north, tracer, feat_out, act_out, w1s, w2s, w3s,
-    ext, landx, feat, act, act0, w1f, w3f, patches, h1, h2, parts, flat, win, mwin, res,
+    depth, b3, u, v, t, land, w1h, w2h, w3h, b1h, b2h,
+    east, north, tracer, feat_out, act_out, w1s, w2s, w3s, b1r, b2r, sel_in, sel_out,
+    ext, landx, feat, act, act0, w1f, w3f, w1, w2, w3, b1, b2, pick,
+    patches, h1, h2, parts, flat, win, mwin, res,
     main_out, edge_out, main_in, edge_in, res_out, res_in,
-    halo_send, halo_recv, win_send, win_recv, res_send, res_recv,
+    load_sem, halo_send, halo_recv, win_send, win_recv, res_send, res_recv,
 ):
     level, tile = lax.axis_index("group"), lax.axis_index("tile")
     tiles = lax.axis_size("tile")
@@ -235,6 +245,25 @@
     across = cols // TS
     mesh_id = pl.DeviceIdType.MESH
 
+    loads = [
+        pltpu.make_async_copy(origin, place, load_sem.at[i])
+        for i, (origin, place) in enumerate(
+            (
+                (u, ext.at[0, pl.ds(16, TS)]),
+                (v, ext.at[1, pl.ds(16, TS)]),
+                (t, ext.at[2, pl.ds(16, TS)]),
+                (land, landx.at[pl.ds(16, TS)]),
+                (w1h, w1),
+                (w2h, w2),
+                (w3h, w3),
+                (b1h, b1),
+                (b2h, b2),
+            )
+        )
+    ]
+    for load in loads:
+        load.start()
+
     barrier = pltpu.get_barrier_semaphore()
 
     def greet(group, place):
@@ -259,6 +288,13 @@
 
     peers = jnp.where(tile > 0, 1, 0) + jnp.where(tile < tiles - 1, 1, 0)
     peers = peers + jnp.where(level == 0, 2, jnp.where(level == 1, 0, 1))
+
+    for f in range(3):
+        ext[f, 0:8, :] = jnp.zeros((8, cols), f32)
+        ext[f, 152:160, :] = jnp.zeros((8, cols), f32)
+    landx[0:8, :] = jnp.zeros((8, cols), jnp.int32)
+    landx[152:160, :] = jnp.zeros((8, cols), jnp.int32)
+    build_tables(sel_in, sel_out, pick)
     pl.semaphore_wait(barrier, peers)
 
     def halo_copy(way, f):
@@ -284,14 +320,6 @@
         for f in range(4):
             halo_copy(1, f).start()
 
-    for f, src in enumerate((u, v, t)):
-        ext[f, 0:8, :] = jnp.zeros((8, cols), f32)
-        ext[f, 152:160, :] = jnp.zeros((8, cols), f32)
-        ext[f, 16:144, :] = src[...]
-    landx[0:8, :] = jnp.zeros((8, cols), jnp.int32)
-    landx[152:160, :] = jnp.zeros((8, cols), jnp.int32)
-    landx[16:144, :] = land[...]
-
     @pl.when(tile == 0)
     def _():
         for f in range(3):
@@ -319,7 +347,37 @@
         rows_of(k, wet_mid, True)
         return carry
 
+    for load in loads[:4]:
+        load.wait()
     lax.fori_loop(1, 15, inner, 0)
+
+    def window_copy(slot, part):
+        group, place = ((2, 0), (3, 0), (3, 1))[slot]
+        if part == 3:
+            src, dst = edge_out.at[slot], edge_in.at[place]
+        else:
+            rows = pl.ds(*((16, 112), (0, 16), (128, 16))[part])
+            src, dst = main_out.at[slot, :, rows], main_in.at[place, :, rows]
+        return pltpu.make_async_remote_copy(
+            src_ref=src,
+            dst_ref=dst,
+            send_sem=win_send.at[slot, part],
+            recv_sem=win_recv.at[place, part],
+            device_id=(group, tile),
+            device_id_type=mesh_id,
+        )
+
+    @pl.when(level == 0)
+    def _():
+        for slot in (1, 0, 2):
+            lane0 = (KEPT + slot) * TS
+            main_out[slot, :, 16:128] = feat[:, 16:128, lane0 : lane0 + TS].astype(bf16)
+            window_copy(slot, 0).start()
+
+    for load in loads[4:]:
+        load.wait()
+    build_weights(w1, w2, w3, b1, b2, w1f, w1s, w2s, w3f, w3s, b1r, b2r)
+    flat[...] = jnp.zeros_like(flat)
 
     @pl.when(tile > 0)
     def _():
@@ -336,32 +394,19 @@
     rows_of(15, wet_mid, True)
     rows_of(16, wet_high, False)
 
-    def window_copy(slot, part):
-        group, place = ((2, 0), (3, 0), (3, 1))[slot]
-        src, dst = ((main_out, main_in), (edge_out, edge_in))[part]
-        return pltpu.make_async_remote_copy(
-            src_ref=src.at[slot],
-            dst_ref=dst.at[place],
-            send_sem=win_send.at[slot, part],
-            recv_sem=win_recv.at[place, part],
-            device_id=(group, tile),
-            device_id_type=mesh_id,
-        )
-
     @pl.when(level == 0)
     def _():
         for slot in (1, 0, 2):
             lane0 = (KEPT + slot) * TS
-            main_out[slot] = feat[:, :, lane0 : lane0 + TS].astype(bf16)
+            for part, rows in ((1, slice(0, 16)), (2, slice(128, 144))):
+                main_out[slot, :, rows] = feat[:, rows, lane0 : lane0 + TS].astype(bf16)
+                window_copy(slot, part).start()
             edge = feat[:, :, lane0 + TS : lane0 + 2 * TS].reshape(432, TS).astype(bf16)
             edge_out[slot] = lax.dot_general(
                 pick[...], edge, (((1,), (1,)), ((), ())), preferred_element_type=f32
             ).astype(bf16)
-            for part in range(2):
-                window_copy(slot, part).start()
-
-    build_weights(w1, w2, w3, w1f, w1s, w2s, w3f, w3s)
-    flat[...] = jnp.zeros_like(flat)
+            window_copy(slot, 3).start()
+
     feat_out[...] = feat[...].astype(bf16)
     act_out[...] = act[...]
 
@@ -385,11 +430,15 @@
 
         @pl.when(level >= 2)
         def _():
-            for part in range(2):
-                src, dst = ((main_out, main_in), (edge_out, edge_in))[part]
+            for part in range(4):
+                if part == 3:
+                    src, dst = edge_out.at[0], edge_in.at[item]
+                else:
+                    rows = pl.ds(*((16, 112), (0, 16), (128, 16))[part])
+                    src, dst = main_out.at[0, :, rows], main_in.at[item, :, rows]
                 pltpu.make_async_remote_copy(
-                    src_ref=src.at[0],
-                    dst_ref=dst.at[item],
+                    src_ref=src,
+                    dst_ref=dst,
                     send_sem=win_send.at[0, part],
                     recv_sem=win_recv.at[item, part],
                     device_id=(0, tile),
@@ -404,7 +453,7 @@
             mwin[...] = act0[:, pl.ds(from0, 2 * TS)]
 
         closure_tile(
-            win, mwin, res, sel_in, sel_out, b1, b2, b3, w1s, w2s, w3s, patches, h1, h2, parts, flat
+            win, mwin, res, sel_in, sel_out, b1r, b2r, b3, w1s, w2s, w3s, patches, h1, h2, parts, flat
         )
 
         @pl.when(level == 0)
@@ -435,7 +484,7 @@
             lane0 = (KEPT + slot) * TS
             east[:, lane0 : lane0 + TS] += res_in[slot, 0]
             north[:, lane0 : lane0 + TS] += res_in[slot, 1]
-            for part in range(2):
+            for part in range(4):
                 window_copy(slot, part).wait_send()
 
     @pl.when(level == 2)
@@ -459,50 +508,60 @@
 
 
 def second_kernel(
-    depth, meta, b3, east1, north1, feat, act, w1s, w2s, w3s, b1, b2, sel_in, sel_out,
-    east, north,
-    patches, h1, h2, parts, flat, win, mwin, res,
+    depth, b3, east1, north1, tracer1, feat, act, w1s, w2s, w3s, b1, b2, sel_in, sel_out,
+    east, north, tracer,
+    sums, patches, h1, h2, parts, flat, win, mwin, res,
+    tracer_sem, out_sem,
 ):
-    level, tile = meta[0], meta[1]
-    across = east.shape[1] // TS
-    east[...] = east1[...]
-    north[...] = north1[...]
-
-    @pl.when(level > 0)
-    def _():
-        flat[...] = jnp.zeros_like(flat)
-
-        def column(ty, carry):
-            @pl.when(depth[tile * across + ty] > level)
-            def _():
-                lane0 = pl.multiple_of(ty * TS, TS)
-                win[...] = feat[:, :, pl.ds(lane0, 2 * TS)].astype(f32)
-                mwin[...] = act[:, pl.ds(lane0, 2 * TS)]
-                closure_tile(
-                    win, mwin, res, sel_in, sel_out, b1, b2, b3, w1s, w2s, w3s,
-                    patches, h1, h2, parts, flat,
-                )
-                add_push(east, north, res, lane0)
-
-            return carry
-
-        lax.fori_loop(0, across, column, 0)
+    level, tile = lax.axis_index("group"), lax.axis_index("tile")
+    across = east1.shape[1] // TS
+    tracer_copy = pltpu.make_async_copy(tracer1, tracer, tracer_sem)
+    tracer_copy.start()
+    sums[0] = east1[...]
+    sums[1] = north1[...]
+    flat[...] = jnp.zeros_like(flat)
+
+    def block_copy(ty, which):
+        lanes = pl.ds(pl.multiple_of(ty * TS, TS), TS)
+        return pltpu.make_async_copy(
+            sums.at[which, :, lanes], (east, north)[which].at[:, lanes], out_sem.at[ty, which]
+        )
+
+    def column(ty, carry):
+        @pl.when((level > 0) & (depth[tile * across + ty] > level))
+        def _():
+            lane0 = pl.multiple_of(ty * TS, TS)
+            win[...] = feat[:, :, pl.ds(lane0, 2 * TS)].astype(f32)
+            mwin[...] = act[:, pl.ds(lane0, 2 * TS)]
+            closure_tile(
+                win, mwin, res, sel_in, sel_out, b1, b2, b3, w1s, w2s, w3s,
+                patches, h1, h2, parts, flat,
+            )
+            for which in range(2):
+                sums[which, :, pl.ds(lane0, TS)] += res[which]
+
+        for which in range(2):
+            block_copy(ty, which).start()
+        return carry
+
+    lax.fori_loop(0, across, column, 0)
+
+    def drain(ty, carry):
+        for which in range(2):
+            block_copy(ty, which).wait()
+        return carry
+
+    lax.fori_loop(0, across, drain, 0)
+    tracer_copy.wait()
 
 
 def body(u, v, t, land, depth, conv_one, bias_one, conv_two, bias_two, conv_three, bias_three):
     levels, rows, cols = u.shape
-    w1 = conv_one.transpose(1, 3, 2, 0).astype(f32)
-    w2 = conv_two.transpose(2, 3, 1, 0).astype(f32)
-    w3 = conv_three.transpose(0, 2, 3, 1).astype(f32)
-    b1 = jnp.tile(0.5 * bias_one, 4)[None]
-    b2 = jnp.tile(0.5 * bias_two, 4)[None]
-    sel_in = jnp.asarray(select_in(), bf16)
-    sel_out = jnp.asarray(select_out(), bf16)
-    pick = jnp.asarray(np.eye(16, TS, dtype=np.float32), bf16)
-    meta = jnp.stack([lax.axis_index("group"), lax.axis_index("tile")]).astype(jnp.int32)
     vmem = pl.BlockSpec(memory_space=pltpu.VMEM)
     smem = pl.BlockSpec(memory_space=pltpu.SMEM)
+    hbm = pl.BlockSpec(memory_space=pltpu.HBM)
     wide = cols + TS
+    across = cols // TS
     plane = jax.ShapeDtypeStruct((rows, cols), f32)
     work = [
         pltpu.VMEM((9, SLAB, TS), bf16),
@@ -514,7 +573,10 @@
         pltpu.VMEM((144, 2 * TS), f32),
         pltpu.VMEM((2, TS, TS), f32),
     ]
-    east1, north1, tracer, feat, act, w1s, w2s, w3s = pl.pallas_call(
+    def stay(x):
+        return pltpu.with_memory_space_constraint(x, pltpu.HBM)
+
+    east1, north1, tracer1, feat, act, w1s, w2s, w3s, b1r, b2r, sel_in, sel_out = pl.pallas_call(
         first_kernel,
         out_shape=[plane] * 3
         + [
@@ -523,9 +585,13 @@
             jax.ShapeDtypeStruct((4, 256, 256), bf16),
             jax.ShapeDtypeStruct((4, 256, 256), bf16),
             jax.ShapeDtypeStruct((64, 256), bf16),
+            jax.ShapeDtypeStruct((1, 256), f32),
+            jax.ShapeDtypeStruct((1, 256), f32),
+            jax.ShapeDtypeStruct((80, 256), bf16),
+            jax.ShapeDtypeStruct((2, 2, SLAB, 256), bf16),
         ],
-        in_specs=[smem] * 2 + [vmem] * 12,
-        out_specs=[vmem] * 8,
+        in_specs=[smem] * 2 + [hbm] * 9,
+        out_specs=[vmem] * 12,
         scratch_shapes=[
             pltpu.VMEM((3, 160, cols), f32),
             pltpu.VMEM((160, cols), jnp.int32),
@@ -534,6 +600,12 @@
             pltpu.VMEM((144, wide), f32),
             pltpu.VMEM((4, 256, 256), f32),
             pltpu.VMEM((64, 256), f32),
+            pltpu.VMEM((3, 3, 3, 64), bf16),
+            pltpu.VMEM((3, 3, 64, 64), bf16),
+            pltpu.VMEM((3, 3, 3, 64), bf16),
+            pltpu.VMEM((1, 64), f32),
+            pltpu.VMEM((1, 64), f32),
+            pltpu.VMEM((16, TS), bf16),
         ]
         + work
         + [
@@ -543,10 +615,11 @@
             pltpu.VMEM((2, 16, 432), bf16),
             pltpu.VMEM((2, 2, TS, TS), f32),
             pltpu.VMEM((3, 2, TS, TS), f32),
+            pltpu.SemaphoreType.DMA((9,)),
             pltpu.SemaphoreType.DMA((2, 4)),
             pltpu.SemaphoreType.DMA((2, 4)),
-            pltpu.SemaphoreType.DMA((3, 2)),
-            pltpu.SemaphoreType.DMA((2, 2)),
+            pltpu.SemaphoreType.DMA((3, 4)),
+            pltpu.SemaphoreType.DMA((2, 4)),
             pltpu.SemaphoreType.DMA((2,)),
             pltpu.SemaphoreType.DMA((3,)),
         ],
@@ -554,16 +627,25 @@
             vmem_limit_bytes=40 * 2**20, collective_id=0, has_side_effects=True
         ),
         name="first",
-    )(depth, bias_three, u[0], v[0], t[0], land, w1, b1, w2, b2, w3, sel_in, sel_out, pick)
-    east, north = pl.pallas_call(
+    )(
+        depth, bias_three, stay(u[0]), stay(v[0]), stay(t[0]), stay(land),
+        stay(conv_one.transpose(1, 2, 3, 0)), stay(conv_two.transpose(2, 3, 0, 1)),
+        stay(conv_three.transpose(0, 2, 3, 1)), stay(bias_one[None]), stay(bias_two[None]),
+    )
+    east, north, tracer = pl.pallas_call(
         second_kernel,
-        out_shape=[plane] * 2,
-        in_specs=[smem] * 3 + [vmem] * 11,
-        out_specs=[vmem] * 2,
-        scratch_shapes=work,
+        out_shape=[plane] * 3,
+        in_specs=[smem] * 2 + [vmem] * 12,
+        out_specs=[hbm] * 3,
+        scratch_shapes=[pltpu.VMEM((2, rows, cols), f32)]
+        + work
+        + [pltpu.SemaphoreType.DMA, pltpu.SemaphoreType.DMA((across, 2))],
         compiler_params=pltpu.CompilerParams(vmem_limit_bytes=40 * 2**20),
         name="second",
-    )(depth, meta, bias_three, east1, north1, feat, act, w1s, w2s, w3s, b1, b2, sel_in, sel_out)
+    )(
+        depth, bias_three, east1, north1, tracer1, feat, act, w1s, w2s, w3s, b1r, b2r,
+        sel_in, sel_out,
+    )
     return east[None], north[None], tracer[None]
 
 

time: 51.9 us -> 43.6 us (0.84)
  local copies, waits for them, and re-layouts: 8.31 us -> 0.67 us
    unnamed x28 -> x4, local copies, waits for them, and re-layouts: 8.14 us -> 0.67 us
where the time goes in v3:
time: 43.6 us; the launch traced here: 43.5 us
  Pallas kernels  42 us (96%)
  between operations  0.82 us (2%)
  local copies, waits for them, and re-layouts  0.67 us (2%)
    pallas_call x1, Pallas kernels, body(): pl.pallas_call(first_kernel, out_shape=[plane] * 3 + [jax.ShapeDtypeStruc...  40.2 us
    pallas_call x1, Pallas kernels, body(): pl.pallas_call(second_kernel, out_shape=[plane] * 3, in_specs=[smem] * 2...  1.83 us

profile of v3, /device:TPU:24, one launch (start us, length us, event | category | flops | bytes accessed | tf_op | source)
XLA Modules:
  0.0 43.5 jit_solution(3594113333850359567)
XLA Ops:
  0.6 0.0 copy-start
  0.6 0.0 copy-start.1
  0.7 0.7 %copy-done = s32[256]{0:T(256)S(1)} copy-done((s32[256]{0:T(256)S(1)}, s32[256]{0:T(256)}, u32[]{:S(2)}) %copy-start) | copy-done | bytes 1048
  1.3 0.0 copy-done.1
  1.3 40.2 %first.1 = (f32[128,1024]{1,0:T(8,128)S(1)}, f32[128,1024]{1,0:T(8,128)S(1)}, f32[128,1024]{1,0:T(8,128)S(1)}, bf16[3,144,1152]{2,1,0:T(8,128)(2,1)S(1)}, f32[14...) custom-call(s32[256]{0:T(256)S(1)} %copy-done, ...), custom_call_target="tpu_custom_call" | custom-call | tf_op jit(solution)/shard_map/first/pallas_call | solution.py:579
  41.5 1.8 %second.1 = (f32[128,1024]{1,0:T(8,128)}, f32[128,1024]{1,0:T(8,128)}, f32[128,1024]{1,0:T(8,128)}) custom-call(s32[256]{0:T(256)S(1)} %copy-done, f32[3]{0:T(128)S(1)} %copy-done.1, f32[128,1024]{1,0:T(8,128)S(1)} %get-tuple-element.18.east1, f32[128,1024]{1,0:T(8,128)S(1)} %get-tuple-element.19.north1, f32[128,1024]{1,0:T(8,128)S(1)} %get-tuple-element.20.tracer1, ...), custom_call_target="tpu_custom_call" | custom-call | tf_op jit(solution)/shard_map/second/pallas_call | solution.py:635
Async XLA Ops:
  0.6 0.7 %copy-start = (s32[256]{0:T(256)S(1)}, s32[256]{0:T(256)}, u32[]{:S(2)}) copy-start(s32[256]{0:T(256)} %depth.3) | copy-start | bytes 3076
  0.6 0.7 %copy-start.1 = (f32[3]{0:T(128)S(1)}, f32[3]{0:T(128)}, u32[]{:S(2)}) copy-start(f32[3]{0:T(128)} %b3.3) | copy-start | bytes 40

commit v4 on v3

--- a/solution.py
+++ b/solution.py
@@ -1,3 +1,5 @@
+import functools
+
 import jax
 import jax.numpy as jnp
 from jax import lax
@@ -17,7 +19,7 @@
 
 TS = 128
 HALO = 5
-ROWS1, ROWS2, ROWS3 = 35, 34, 33
+ROWS1, ROWS2 = 35, 34
 SLAB = 160
 USED = 144
 
@@ -26,13 +28,13 @@
     row = lax.broadcasted_iota(jnp.int32, (80, 256), 0)
     col = lax.broadcasted_iota(jnp.int32, (80, 256), 1)
     sel_in[...] = (col == 2 * (9 * (row % 8) + row // 8)).astype(f32).astype(bf16)
-    row = lax.broadcasted_iota(jnp.int32, (160, 256), 0)
-    col = lax.broadcasted_iota(jnp.int32, (160, 256), 1)
+    row = lax.broadcasted_iota(jnp.int32, (USED, 256), 0)
+    col = lax.broadcasted_iota(jnp.int32, (USED, 256), 1)
     place = 2 * (9 * (row % 8) + row // 16)
-    inside = (row < USED) & (col < 130)
+    inside = place + 1 < 130
     for ip in range(2):
         for b in range(2):
-            hit = inside & ((row % 16) // 8 == ip) & (col == place + b)
+            hit = inside & ((row % 16) // 8 == ip) & (col == (place + b + 255) % 256)
             sel_out[ip, b] = hit.astype(f32).astype(bf16)
     row = lax.broadcasted_iota(jnp.int32, (16, TS), 0)
     col = lax.broadcasted_iota(jnp.int32, (16, TS), 1)
@@ -81,7 +83,17 @@
                     lane = (ai * 2 + bi) * 64
                     row = (di * 2 + dj) * 16 + bo * 6 + c * 2 + ao
                     w3f[row : row + 1, lane : lane + 64] = line[ky : ky + 1]
-    w3s[...] = w3f[...].astype(bf16)
+    turned = w3f[...].T.astype(bf16)
+    row = lax.broadcasted_iota(jnp.int32, (64, 256), 0)
+    col = lax.broadcasted_iota(jnp.int32, (64, 256), 1)
+    part = row % 16
+    di, dj = row // 32, (row // 16) % 2
+    b, c, a = part // 6, (part % 6) // 2, part % 2
+    for j in range(8):
+        into = jnp.where(j - di >= 0, c * 16 + 2 * (j - di), 48 + 2 * c)
+        hit = (part < 12) & (col == dj * 128 + b * 64 + into + a)
+        spread = jnp.dot(turned, hit.astype(f32).astype(bf16), preferred_element_type=f32)
+        w3s[256 * j : 256 * j + 256, :] = spread.astype(bf16)
     for j in range(4):
         b1r[:, 64 * j : 64 * j + 64] = 0.5 * b1[...]
         b2r[:, 64 * j : 64 * j + 64] = 0.5 * b2[...]
@@ -156,86 +168,124 @@
     ref[index, USED:SLAB, :] = pltpu.roll(value[0:16], 15, 0).astype(bf16)
 
 
-def closure_tile(win, mwin, res, sel_in, sel_out, b1, b2, b3, w1s, w2s, w3s, patches, h1, h2, parts, flat):
-    for g in range(9):
+def closure_pieces(tables, weights, work, b3, read_rows, read_mask, put):
+    sel_in, sel_out = tables
+    w1s, w2s, w3s, b1, b2 = weights
+    patches, h1, h2, parts, flat, image = work
+
+    def gather(g):
         halves = []
         for ip in range(2):
-            base = 64 * ip + 8 * g
-            rows = win[:, base : base + 16, :].reshape(48, 256)
+            rows = read_rows(64 * ip + 8 * g).reshape(48, 256)
             rows = jnp.concatenate([rows, pltpu.roll(rows, 255, 1), jnp.zeros((32, 256), f32)], axis=0)
             got = lax.dot_general(
                 sel_in[...], rows.astype(bf16), (((1,), (1,)), ((), ())), preferred_element_type=f32
             )
             halves.append(got.reshape(10, 8, 128))
-        patches[g] = jnp.stack(halves, axis=1).reshape(SLAB, 128).astype(bf16)
-    for q in range(4):
-        for g in range(9):
-            if 4 * g + q >= ROWS1:
-                continue
-            lhs = jnp.concatenate([patches[g, 0:USED, :], patches[g, 16:SLAB, :]], axis=1)
-            half = jnp.dot(lhs, w1s[q], preferred_element_type=f32) + b1[...]
-            store_slab(h1, 4 * g + q, silu_half(half))
-    for i in range(0, ROWS2, 2):
+        both = jnp.stack(halves, axis=1).reshape(SLAB, 128).astype(bf16)
+        patches[g, :, 0:128] = both[0:USED]
+        patches[g, :, 128:256] = both[16:SLAB]
+
+    def first(q, start):
+        count = 3 if 4 * (start + 2) + q < ROWS1 else 2
+        lhs = patches[start : start + count].reshape(count * USED, 256)
+        half = jnp.dot(lhs, w1s[q], preferred_element_type=f32) + b1[...]
+        out = silu_half(half)
+        for g in range(count):
+            store_slab(h1, 4 * (start + g) + q, out[g * USED : (g + 1) * USED])
+
+    def second(i):
         half = b2[...]
         for di in range(2):
             for dj in range(2):
                 lhs = h1[i + di : i + di + 2, 16 * dj : 16 * dj + USED, :].reshape(2 * USED, 256)
                 half = half + jnp.dot(lhs, w2s[2 * di + dj], preferred_element_type=f32)
-        out = silu_half(half)
-        store_slab(h2, i, out[0:USED])
-        store_slab(h2, i + 1, out[USED:])
-    for i in range(ROWS2):
-        parts[i] = lax.dot_general(
-            w3s[...], h2[i], (((1,), (1,)), ((), ())), preferred_element_type=f32
-        )
-    for i in range(ROWS3):
-        got = (
-            parts[i, 0:16, 0:USED]
-            + parts[i, 16:32, 16:SLAB]
-            + parts[i + 1, 32:48, 0:USED]
-            + parts[i + 1, 48:64, 16:SLAB]
-        )
+        out = silu_half(half).astype(bf16)
+        m, j = i // 8, i % 8
+        h2[m, :, 256 * j : 256 * j + 256] = out[0:USED]
+        h2[m, :, 256 * j + 256 : 256 * j + 512] = out[USED:]
+
+    def third(m):
+        depth = 2048 if m < 4 else 512
+        got = jnp.dot(h2[m, :, 0:depth], w3s[0:depth, :], preferred_element_type=f32)
+        here, later = got[:, 0:128], got[:, 128:256]
+        later = jnp.concatenate([later[16:USED], pltpu.roll(later[0:16], 15, 0)], axis=0)
+        parts[m] = (here + later).T
+
+    def settle(m):
         for b in range(2):
             for c in range(3):
-                r = b * 6 + c * 2
-                flat[b, c, 2 * i : 2 * i + 2, 0:USED] = got[r : r + 2] + b3[c]
-    for ip in range(2):
-        mask = mwin[8 + 64 * ip - 1 : 8 + 64 * ip + 65, :]
-        masked = []
-        for c in range(3):
-            image = jnp.zeros((72, 256), f32)
-            for b in range(2):
-                image = image + jnp.dot(
-                    flat[b, c].astype(bf16), sel_out[ip, b], preferred_element_type=f32
-                )
-            masked.append(image[0:66] * mask)
-        xx, xy, yy = masked
+                at = b * 64 + c * 16
+                rows = parts[m, at : at + 16, :]
+                if m < 4:
+                    rest = parts[m + 1, b * 64 + 48 + 2 * c : b * 64 + 50 + 2 * c, :]
+                    rows = rows + jnp.concatenate([jnp.zeros((14, USED), f32), rest], axis=0)
+                flat[b, 48 * m + 16 * c : 48 * m + 16 * c + 16, :] = (rows + b3[c]).astype(bf16)
+
+    def unfold(ip):
+        rows = 192 + 48 * ip
+        whole = jnp.dot(flat[0, 0:rows], sel_out[ip, 0], preferred_element_type=f32) + jnp.dot(
+            flat[1, 0:rows], sel_out[ip, 1], preferred_element_type=f32
+        )
+        for m in range(4 + ip):
+            for c in range(3):
+                row = 64 * ip + 16 * m
+                image[c, row : row + 16, :] = whole[48 * m + 16 * c : 48 * m + 16 * c + 16]
+
+    def push():
+        mask = pltpu.roll(read_mask(), 255, 1)
+        xx, xy, yy = [image[c, 0:130, :] * mask for c in range(3)]
 
         def dx(m):
-            return 0.5 * (m[2:66, 1:129] - m[0:64, 1:129])
+            return m[2:130, 0:TS] - m[0:128, 0:TS]
 
         def dy(m):
-            return 0.5 * (m[1:65, 2:130] - m[1:65, 0:128])
-
-        gain = eddy_gain * mask[1:65, 1:129]
-        rows = slice(64 * ip, 64 * ip + 64)
-        res[0, rows, :] = gain * (dx(xx) + dy(xy))
-        res[1, rows, :] = gain * (dx(xy) + dy(yy))
-
-
-def add_push(east, north, res, lane0):
-    east[:, pl.ds(lane0, TS)] += res[0]
-    north[:, pl.ds(lane0, TS)] += res[1]
+            mid = m[1:129]
+            return pltpu.roll(mid, 255, 1)[:, 0:TS] - pltpu.roll(mid, 1, 1)[:, 0:TS]
+
+        gain = (0.5 * eddy_gain) * mask[1:129, 0:TS]
+        put(gain * (dx(xx) + dy(xy)), gain * (dx(xy) + dy(yy)))
+
+    gathers = [functools.partial(gather, g) for g in range(9)]
+    firsts = [functools.partial(first, q, start) for q in range(4) for start in range(0, 9, 3)]
+    seconds = [functools.partial(second, i) for i in range(0, ROWS2, 2)]
+    thirds = [functools.partial(third, m) for m in range(5)]
+    rest = [functools.partial(settle, m) for m in range(5)]
+    rest += [functools.partial(unfold, ip) for ip in range(2)] + [push]
+    return gathers, firsts, seconds, thirds, rest
+
+
+def run_all(*lists):
+    for pieces in lists:
+        for piece in pieces:
+            piece()
+
+
+def run_woven(gathers, firsts, seconds, thirds, rest):
+    beside = {}
+    for g, piece in enumerate(gathers):
+        beside.setdefault(GATHER_AT[g], []).append(piece)
+    for n, piece in enumerate(rest):
+        beside.setdefault(REST_AT[n], []).append(piece)
+    run_all(firsts)
+    for i, piece in enumerate(seconds):
+        piece()
+        run_all(beside.get(i, []))
+    run_all(thirds)
+
+
+GATHER_AT = (7, 8, 9, 10, 11, 12, 13, 14, 15)
+REST_AT = (0, 1, 2, 3, 4, 5, 6, 8)
 
 
 KEPT = 5
 
 
 def first_kernel(
-    depth, b3, u, v, t, land, w1h, w2h, w3h, b1h, b2h,
-    east, north, tracer, feat_out, act_out, w1s, w2s, w3s, b1r, b2r, sel_in, sel_out,
-    ext, landx, feat, act, act0, w1f, w3f, w1, w2, w3, b1, b2, pick,
-    patches, h1, h2, parts, flat, win, mwin, res,
+    depth_h, b3_h, u, v, t, land, w1h, w2h, w3h, b1h, b2h,
+    east, north, tracer, feat, act, w1s, w2s, w3s, b1r, b2r, sel_in, sel_out,
+    depth, b3, ext, landx, act0, w1f, w3f, w1, w2, w3, b1, b2, pick,
+    patches, h1, h2, parts, flat, image, win,
     main_out, edge_out, main_in, edge_in, res_out, res_in,
     load_sem, halo_send, halo_recv, win_send, win_recv, res_send, res_recv,
 ):
@@ -249,15 +299,17 @@
         pltpu.make_async_copy(origin, place, load_sem.at[i])
         for i, (origin, place) in enumerate(
             (
-                (u, ext.at[0, pl.ds(16, TS)]),
-                (v, ext.at[1, pl.ds(16, TS)]),
-                (t, ext.at[2, pl.ds(16, TS)]),
-                (land, landx.at[pl.ds(16, TS)]),
                 (w1h, w1),
                 (w2h, w2),
                 (w3h, w3),
                 (b1h, b1),
                 (b2h, b2),
+                (b3_h, b3),
+                (depth_h, depth),
+                (u, ext.at[0, pl.ds(16, TS)]),
+                (v, ext.at[1, pl.ds(16, TS)]),
+                (t, ext.at[2, pl.ds(16, TS)]),
+                (land, landx.at[pl.ds(16, TS)]),
             )
         )
     ]
@@ -294,7 +346,6 @@
         ext[f, 152:160, :] = jnp.zeros((8, cols), f32)
     landx[0:8, :] = jnp.zeros((8, cols), jnp.int32)
     landx[152:160, :] = jnp.zeros((8, cols), jnp.int32)
-    build_tables(sel_in, sel_out, pick)
     pl.semaphore_wait(barrier, peers)
 
     def halo_copy(way, f):
@@ -332,6 +383,10 @@
             ext[f, 144:152, :] = jnp.zeros((8, cols), f32)
         landx[144:152, :] = jnp.zeros((8, cols), jnp.int32)
 
+    build_tables(sel_in, sel_out, pick)
+    for load in loads[:7]:
+        load.wait()
+    build_weights(w1, w2, w3, b1, b2, w1f, w1s, w2s, w3f, w3s, b1r, b2r)
     lane = lax.broadcasted_iota(jnp.int32, (8, cols), 1)
     rows_all = float(tiles * TS)
     wet_mid = wet_line(depth, level, tile, lane, across)
@@ -347,7 +402,7 @@
         rows_of(k, wet_mid, True)
         return carry
 
-    for load in loads[:4]:
+    for load in loads[7:]:
         load.wait()
     lax.fori_loop(1, 15, inner, 0)
 
@@ -374,10 +429,6 @@
             main_out[slot, :, 16:128] = feat[:, 16:128, lane0 : lane0 + TS].astype(bf16)
             window_copy(slot, 0).start()
 
-    for load in loads[4:]:
-        load.wait()
-    build_weights(w1, w2, w3, b1, b2, w1f, w1s, w2s, w3f, w3s, b1r, b2r)
-    flat[...] = jnp.zeros_like(flat)
 
     @pl.when(tile > 0)
     def _():
@@ -407,8 +458,6 @@
             ).astype(bf16)
             window_copy(slot, 3).start()
 
-    feat_out[...] = feat[...].astype(bf16)
-    act_out[...] = act[...]
 
     def result_copy(item):
         return pltpu.make_async_remote_copy(
@@ -420,16 +469,39 @@
             device_id_type=mesh_id,
         )
 
-    def item_step(item, carry):
-        lane0 = pl.multiple_of(item * TS, TS)
-
-        @pl.when(level == 0)
-        def _():
-            win[...] = feat[:, :, pl.ds(lane0, 2 * TS)]
-            mwin[...] = act[:, pl.ds(lane0, 2 * TS)]
-
-        @pl.when(level >= 2)
-        def _():
+    tables, weights = (sel_in, sel_out), (w1s, w2s, w3s, b1r, b2r)
+    work = (patches, h1, h2, parts, flat, image)
+
+    def own_pieces(next_item, last_item):
+        next_lane = pl.multiple_of(next_item * TS, TS)
+        last_lane = pl.multiple_of(jnp.where(last_item < 0, 0, last_item) * TS, TS)
+
+        def put(push_east, push_north):
+            for ref, push in ((east, push_east), (north, push_north)):
+                ref[:, pl.ds(last_lane, TS)] += jnp.where(last_item < 0, 0.0, push)
+
+        return closure_pieces(
+            tables, weights, work, b3,
+            lambda base: feat[:, pl.ds(base, 16), pl.ds(next_lane, 2 * TS)],
+            lambda: act[7:137, pl.ds(last_lane, 2 * TS)],
+            put,
+        )
+
+    @pl.when(level == 0)
+    def _():
+        parts[...] = jnp.zeros_like(parts)
+        run_all(own_pieces(0, 0)[0])
+
+        def item_step(item, carry):
+            run_woven(*own_pieces(item + 1, item - 1))
+            return carry
+
+        lax.fori_loop(0, KEPT, item_step, 0)
+        run_all(own_pieces(0, KEPT - 1)[4])
+
+    @pl.when(level >= 2)
+    def _():
+        def item_step(item, carry):
             for part in range(4):
                 if part == 3:
                     src, dst = edge_out.at[0], edge_in.at[item]
@@ -450,25 +522,23 @@
             )
             win[:, :, TS : 2 * TS] = edge.reshape(3, 144, TS)
             from0 = pl.multiple_of((KEPT + level - 2 + item) * TS, TS)
-            mwin[...] = act0[:, pl.ds(from0, 2 * TS)]
-
-        closure_tile(
-            win, mwin, res, sel_in, sel_out, b1r, b2r, b3, w1s, w2s, w3s, patches, h1, h2, parts, flat
-        )
-
-        @pl.when(level == 0)
-        def _():
-            add_push(east, north, res, lane0)
-
-        @pl.when(level >= 2)
-        def _():
-            res_out[item] = res[...]
+
+            def put(push_east, push_north):
+                res_out[item, 0] = push_east
+                res_out[item, 1] = push_north
+
+            run_all(
+                *closure_pieces(
+                    tables, weights, work, b3,
+                    lambda base: win[:, base : base + 16, :],
+                    lambda: act0[7:137, pl.ds(from0, 2 * TS)],
+                    put,
+                )
+            )
             result_copy(item).start()
-
-        return carry
-
-    here = jnp.where(level == 0, KEPT, jnp.where(level == 1, 0, level - 1))
-    lax.fori_loop(0, here, item_step, 0)
+            return carry
+
+        lax.fori_loop(0, level - 1, item_step, 0)
 
     @pl.when(level == 0)
     def _():
@@ -508,18 +578,25 @@
 
 
 def second_kernel(
-    depth, b3, east1, north1, tracer1, feat, act, w1s, w2s, w3s, b1, b2, sel_in, sel_out,
+    depth_h, b3_h, east1, north1, tracer1, feat, act, w1s, w2s, w3s, b1, b2, sel_in, sel_out,
     east, north, tracer,
-    sums, patches, h1, h2, parts, flat, win, mwin, res,
-    tracer_sem, out_sem,
+    depth, b3, columns, sums, patches, h1, h2, parts, flat, image,
+    load_sem, tracer_sem, out_sem,
 ):
     level, tile = lax.axis_index("group"), lax.axis_index("tile")
     across = east1.shape[1] // TS
     tracer_copy = pltpu.make_async_copy(tracer1, tracer, tracer_sem)
+    loads = [
+        pltpu.make_async_copy(b3_h, b3, load_sem.at[0]),
+        pltpu.make_async_copy(depth_h, depth, load_sem.at[1]),
+    ]
+    for load in loads:
+        load.start()
     tracer_copy.start()
     sums[0] = east1[...]
     sums[1] = north1[...]
-    flat[...] = jnp.zeros_like(flat)
+    for load in loads:
+        load.wait()
 
     def block_copy(ty, which):
         lanes = pl.ds(pl.multiple_of(ty * TS, TS), TS)
@@ -527,24 +604,52 @@
             sums.at[which, :, lanes], (east, north)[which].at[:, lanes], out_sem.at[ty, which]
         )
 
-    def column(ty, carry):
-        @pl.when((level > 0) & (depth[tile * across + ty] > level))
-        def _():
-            lane0 = pl.multiple_of(ty * TS, TS)
-            win[...] = feat[:, :, pl.ds(lane0, 2 * TS)].astype(f32)
-            mwin[...] = act[:, pl.ds(lane0, 2 * TS)]
-            closure_tile(
-                win, mwin, res, sel_in, sel_out, b1, b2, b3, w1s, w2s, w3s,
-                patches, h1, h2, parts, flat,
-            )
-            for which in range(2):
-                sums[which, :, pl.ds(lane0, TS)] += res[which]
-
+    def send(ty):
         for which in range(2):
             block_copy(ty, which).start()
-        return carry
-
-    lax.fori_loop(0, across, column, 0)
+
+    count = jnp.int32(0)
+    for ty in range(across):
+        mine = (level > 0) & (depth[tile * across + ty] > level)
+        columns[count] = jnp.int32(ty)
+        count = count + mine.astype(jnp.int32)
+
+        @pl.when(jnp.logical_not(mine))
+        def _():
+            send(ty)
+
+    def own_pieces(next_item, last_item):
+        next_lane = pl.multiple_of(columns[next_item] * TS, TS)
+        last_lane = pl.multiple_of(columns[jnp.maximum(last_item, 0)] * TS, TS)
+
+        def put(push_east, push_north):
+            for which, push in ((0, push_east), (1, push_north)):
+                sums[which, :, pl.ds(last_lane, TS)] += jnp.where(last_item < 0, 0.0, push)
+
+        return closure_pieces(
+            (sel_in, sel_out), (w1s, w2s, w3s, b1, b2), (patches, h1, h2, parts, flat, image), b3,
+            lambda base: feat[:, pl.ds(base, 16), pl.ds(next_lane, 2 * TS)],
+            lambda: act[7:137, pl.ds(last_lane, 2 * TS)],
+            put,
+        )
+
+    @pl.when(count > 0)
+    def _():
+        parts[...] = jnp.zeros_like(parts)
+        run_all(own_pieces(0, 0)[0])
+
+        def item_step(item, carry):
+            run_woven(*own_pieces(jnp.minimum(item + 1, count - 1), item - 1))
+
+            @pl.when(item > 0)
+            def _():
+                send(columns[item - 1])
+
+            return carry
+
+        lax.fori_loop(0, count, item_step, 0)
+        run_all(own_pieces(0, count - 1)[4])
+        send(columns[count - 1])
 
     def drain(ty, carry):
         for which in range(2):
@@ -558,20 +663,17 @@
 def body(u, v, t, land, depth, conv_one, bias_one, conv_two, bias_two, conv_three, bias_three):
     levels, rows, cols = u.shape
     vmem = pl.BlockSpec(memory_space=pltpu.VMEM)
-    smem = pl.BlockSpec(memory_space=pltpu.SMEM)
     hbm = pl.BlockSpec(memory_space=pltpu.HBM)
     wide = cols + TS
     across = cols // TS
     plane = jax.ShapeDtypeStruct((rows, cols), f32)
     work = [
-        pltpu.VMEM((9, SLAB, TS), bf16),
+        pltpu.VMEM((9, USED, 256), bf16),
         pltpu.VMEM((ROWS1 + 1, SLAB, 256), bf16),
-        pltpu.VMEM((ROWS2, SLAB, 256), bf16),
-        pltpu.VMEM((ROWS2, 64, SLAB), f32),
-        pltpu.VMEM((2, 3, 72, SLAB), f32),
-        pltpu.VMEM((3, 144, 2 * TS), f32),
-        pltpu.VMEM((144, 2 * TS), f32),
-        pltpu.VMEM((2, TS, TS), f32),
+        pltpu.VMEM((5, USED, 2048), bf16),
+        pltpu.VMEM((5, TS, USED), f32),
+        pltpu.VMEM((2, 240, USED), bf16),
+        pltpu.VMEM((3, 144, 256), f32),
     ]
     def stay(x):
         return pltpu.with_memory_space_constraint(x, pltpu.HBM)
@@ -580,23 +682,23 @@
         first_kernel,
         out_shape=[plane] * 3
         + [
-            jax.ShapeDtypeStruct((3, 144, wide), bf16),
+            jax.ShapeDtypeStruct((3, 144, wide), f32),
             jax.ShapeDtypeStruct((144, wide), f32),
             jax.ShapeDtypeStruct((4, 256, 256), bf16),
             jax.ShapeDtypeStruct((4, 256, 256), bf16),
-            jax.ShapeDtypeStruct((64, 256), bf16),
+            jax.ShapeDtypeStruct((2048, 256), bf16),
             jax.ShapeDtypeStruct((1, 256), f32),
             jax.ShapeDtypeStruct((1, 256), f32),
             jax.ShapeDtypeStruct((80, 256), bf16),
-            jax.ShapeDtypeStruct((2, 2, SLAB, 256), bf16),
+            jax.ShapeDtypeStruct((2, 2, USED, 256), bf16),
         ],
-        in_specs=[smem] * 2 + [hbm] * 9,
+        in_specs=[hbm] * 11,
         out_specs=[vmem] * 12,
         scratch_shapes=[
+            pltpu.SMEM(depth.shape, jnp.int32),
+            pltpu.SMEM((3,), f32),
             pltpu.VMEM((3, 160, cols), f32),
             pltpu.VMEM((160, cols), jnp.int32),
-            pltpu.VMEM((3, 144, wide), f32),
-            pltpu.VMEM((144, wide), f32),
             pltpu.VMEM((144, wide), f32),
             pltpu.VMEM((4, 256, 256), f32),
             pltpu.VMEM((64, 256), f32),
@@ -609,13 +711,14 @@
         ]
         + work
         + [
+            pltpu.VMEM((3, 144, 2 * TS), f32),
             pltpu.VMEM((3, 3, 144, TS), bf16),
             pltpu.VMEM((3, 16, 432), bf16),
             pltpu.VMEM((2, 3, 144, TS), bf16),
             pltpu.VMEM((2, 16, 432), bf16),
             pltpu.VMEM((2, 2, TS, TS), f32),
             pltpu.VMEM((3, 2, TS, TS), f32),
-            pltpu.SemaphoreType.DMA((9,)),
+            pltpu.SemaphoreType.DMA((11,)),
             pltpu.SemaphoreType.DMA((2, 4)),
             pltpu.SemaphoreType.DMA((2, 4)),
             pltpu.SemaphoreType.DMA((3, 4)),
@@ -628,22 +731,27 @@
         ),
         name="first",
     )(
-        depth, bias_three, stay(u[0]), stay(v[0]), stay(t[0]), stay(land),
+        stay(depth), stay(bias_three), stay(u[0]), stay(v[0]), stay(t[0]), stay(land),
         stay(conv_one.transpose(1, 2, 3, 0)), stay(conv_two.transpose(2, 3, 0, 1)),
         stay(conv_three.transpose(0, 2, 3, 1)), stay(bias_one[None]), stay(bias_two[None]),
     )
     east, north, tracer = pl.pallas_call(
         second_kernel,
         out_shape=[plane] * 3,
-        in_specs=[smem] * 2 + [vmem] * 12,
+        in_specs=[hbm] * 2 + [vmem] * 12,
         out_specs=[hbm] * 3,
-        scratch_shapes=[pltpu.VMEM((2, rows, cols), f32)]
+        scratch_shapes=[
+            pltpu.SMEM(depth.shape, jnp.int32),
+            pltpu.SMEM((3,), f32),
+            pltpu.SMEM((across,), jnp.int32),
+            pltpu.VMEM((2, rows, cols), f32),
+        ]
         + work
-        + [pltpu.SemaphoreType.DMA, pltpu.SemaphoreType.DMA((across, 2))],
+        + [pltpu.SemaphoreType.DMA((2,)), pltpu.SemaphoreType.DMA, pltpu.SemaphoreType.DMA((across, 2))],
         compiler_params=pltpu.CompilerParams(vmem_limit_bytes=40 * 2**20),
         name="second",
     )(
-        depth, bias_three, east1, north1, tracer1, feat, act, w1s, w2s, w3s, b1r, b2r,
+        stay(depth), stay(bias_three), east1, north1, tracer1, feat, act, w1s, w2s, w3s, b1r, b2r,
         sel_in, sel_out,
     )
     return east[None], north[None], tracer[None]

time: 43.6 us -> 39.3 us (0.901)
  Pallas kernels: 42 us -> 38.4 us
  local copies, waits for them, and re-layouts: 0.67 us -> 0 us
    pallas_call x1, Pallas kernels: 40.2 us -> 36.6 us  [body(): pl.pallas_call(first_kernel, out_shape=[plane] * 3 + [jax.ShapeDtypeStruc...]
    unnamed x4 -> x0, local copies, waits for them, and re-layouts: 0.67 us -> none
where the time goes in v4:
time: 39.3 us; the launch traced here: 39.2 us
  Pallas kernels  38.4 us (98%)
  between operations  0.82 us (2%)
    pallas_call x1, Pallas kernels, body(): pl.pallas_call(first_kernel, out_shape=[plane] * 3 + [jax.ShapeDtypeStruc...  36.6 us
    pallas_call x1, Pallas kernels, body(): pl.pallas_call(second_kernel, out_shape=[plane] * 3, in_specs=[hbm] * 2 +...  1.83 us

profile of v4, /device:TPU:24, one launch (start us, length us, event | category | flops | bytes accessed | tf_op | source)
XLA Modules:
  0.0 39.2 jit_solution(3546246161874214996)
XLA Ops:
  0.6 36.6 %first.1 = (f32[128,1024]{1,0:T(8,128)S(1)}, f32[128,1024]{1,0:T(8,128)S(1)}, f32[128,1024]{1,0:T(8,128)S(1)}, f32[3,144,1152]{2,1,0:T(8,128)S(1)}, f32[144,1152...) custom-call(s32[256]{0:T(256)} %depth_h.3, ...), custom_call_target="tpu_custom_call" | custom-call | tf_op jit(solution)/shard_map/first/pallas_call | solution.py:681
  37.2 1.8 %second.1 = (f32[128,1024]{1,0:T(8,128)}, f32[128,1024]{1,0:T(8,128)}, f32[128,1024]{1,0:T(8,128)}) custom-call(s32[256]{0:T(256)} %depth_h.3, f32[3]{0:T(128)} %b3_h.3, f32[128,1024]{1,0:T(8,128)S(1)} %get-tuple-element.18.east1, f32[128,1024]{1,0:T(8,128)S(1)} %get-tuple-element.19.north1, f32[128,1024]{1,0:T(8,128)S(1)} %get-tuple-element.20.tracer1, ...), custom_call_target="tpu_custom_call" | custom-call | tf_op jit(solution)/shard_map/second/pallas_call | solution.py:738

commit v5 on v4

--- a/solution.py
+++ b/solution.py
@@ -120,15 +120,11 @@
         return jnp.where(lane == cols - 1, 0.0, pltpu.roll(x, cols - 1, 1))
 
     base = 8 * k + 16
-    if not isinstance(k, int):
-        base = pl.multiple_of(base, 8)
-    water = jnp.where(landx[pl.ds(base, 8), :] == 1, 1.0, 0.0)
+    water = jnp.where(landx[base : base + 8, :] == 1, 1.0, 0.0)
     active = water * wet
-    above = base - 8 if isinstance(k, int) else pl.multiple_of(base - 8, 8)
-    around = [ext[f, pl.ds(above, 24), :] for f in range(3)]
-    mid = [x[8:16] for x in around]
-    up = [x[7:15] for x in around]
-    down = [x[9:17] for x in around]
+    mid = [ext[f, base : base + 8, :] for f in range(3)]
+    up = [ext[f, base - 1 : base + 7, :] for f in range(3)]
+    down = [ext[f, base + 1 : base + 9, :] for f in range(3)]
     left = [west(x) for x in mid]
     right = [east_of(x) for x in mid]
     lap = [down[f] + up[f] + right[f] + left[f] - 4.0 * mid[f] for f in range(3)]
@@ -144,14 +140,10 @@
     )
     if store:
         at = 8 * k
-        if not isinstance(k, int):
-            at = pl.multiple_of(at, 8)
         east[pl.ds(at, 8), :] = new_east
         north[pl.ds(at, 8), :] = new_north
         tracer[pl.ds(at, 8), :] = new_tracer
     q = 8 * k + 8
-    if not isinstance(k, int):
-        q = pl.multiple_of(q, 8)
     for c, new in enumerate((new_east, new_north, new_tracer)):
         wide = jnp.concatenate([new * active, zeros], axis=1)
         feat[c, pl.ds(q, 8), :] = pltpu.roll(wide, 4, 1)
@@ -384,9 +376,8 @@
         landx[144:152, :] = jnp.zeros((8, cols), jnp.int32)
 
     build_tables(sel_in, sel_out, pick)
-    for load in loads[:7]:
+    for load in loads[5:7]:
         load.wait()
-    build_weights(w1, w2, w3, b1, b2, w1f, w1s, w2s, w3f, w3s, b1r, b2r)
     lane = lax.broadcasted_iota(jnp.int32, (8, cols), 1)
     rows_all = float(tiles * TS)
     wet_mid = wet_line(depth, level, tile, lane, across)
@@ -398,13 +389,10 @@
             k, tile, rows_all, wet, ext, landx, east, north, tracer, feat, act, act0, store
         )
 
-    def inner(k, carry):
-        rows_of(k, wet_mid, True)
-        return carry
-
     for load in loads[7:]:
         load.wait()
-    lax.fori_loop(1, 15, inner, 0)
+    for k in range(1, 15):
+        rows_of(k, wet_mid, True)
 
     def window_copy(slot, part):
         group, place = ((2, 0), (3, 0), (3, 1))[slot]
@@ -428,6 +416,10 @@
             lane0 = (KEPT + slot) * TS
             main_out[slot, :, 16:128] = feat[:, 16:128, lane0 : lane0 + TS].astype(bf16)
             window_copy(slot, 0).start()
+
+    for load in loads[:5]:
+        load.wait()
+    build_weights(w1, w2, w3, b1, b2, w1f, w1s, w2s, w3f, w3s, b1r, b2r)
 
 
     @pl.when(tile > 0)
@@ -524,8 +516,8 @@
             from0 = pl.multiple_of((KEPT + level - 2 + item) * TS, TS)
 
             def put(push_east, push_north):
-                res_out[item, 0] = push_east
-                res_out[item, 1] = push_north
+                res_out[item, 0] = push_east.astype(bf16)
+                res_out[item, 1] = push_north.astype(bf16)
 
             run_all(
                 *closure_pieces(
@@ -552,8 +544,8 @@
                 device_id_type=mesh_id,
             ).wait_recv()
             lane0 = (KEPT + slot) * TS
-            east[:, lane0 : lane0 + TS] += res_in[slot, 0]
-            north[:, lane0 : lane0 + TS] += res_in[slot, 1]
+            east[:, lane0 : lane0 + TS] += res_in[slot, 0].astype(f32)
+            north[:, lane0 : lane0 + TS] += res_in[slot, 1].astype(f32)
             for part in range(4):
                 window_copy(slot, part).wait_send()
 
@@ -716,8 +708,8 @@
             pltpu.VMEM((3, 16, 432), bf16),
             pltpu.VMEM((2, 3, 144, TS), bf16),
             pltpu.VMEM((2, 16, 432), bf16),
-            pltpu.VMEM((2, 2, TS, TS), f32),
-            pltpu.VMEM((3, 2, TS, TS), f32),
+            pltpu.VMEM((2, 2, TS, TS), bf16),
+            pltpu.VMEM((3, 2, TS, TS), bf16),
             pltpu.SemaphoreType.DMA((11,)),
             pltpu.SemaphoreType.DMA((2, 4)),
             pltpu.SemaphoreType.DMA((2, 4)),

time: 39.3 us -> 39.4 us (level)
  no operation moved by 1% of the time
where the time goes in v5:
time: 39.4 us; the launch traced here: 39.3 us
  Pallas kernels  38.4 us (97%)
  between operations  0.82 us (2%)
    pallas_call x1, Pallas kernels, body(): pl.pallas_call(first_kernel, out_shape=[plane] * 3 + [jax.ShapeDtypeStruc...  36.6 us
    pallas_call x1, Pallas kernels, body(): pl.pallas_call(second_kernel, out_shape=[plane] * 3, in_specs=[hbm] * 2 +...  1.83 us

profile of v5, /device:TPU:24, one launch (start us, length us, event | category | flops | bytes accessed | tf_op | source)
XLA Modules:
  0.0 39.3 jit_solution(10158325767433505243)
XLA Ops:
  0.6 36.6 %first.1 = (f32[128,1024]{1,0:T(8,128)S(1)}, f32[128,1024]{1,0:T(8,128)S(1)}, f32[128,1024]{1,0:T(8,128)S(1)}, f32[3,144,1152]{2,1,0:T(8,128)S(1)}, f32[144,1152...) custom-call(s32[256]{0:T(256)} %depth_h.3, ...), custom_call_target="tpu_custom_call" | custom-call | tf_op jit(solution)/shard_map/first/pallas_call | solution.py:673
  37.2 1.8 %second.1 = (f32[128,1024]{1,0:T(8,128)}, f32[128,1024]{1,0:T(8,128)}, f32[128,1024]{1,0:T(8,128)}) custom-call(s32[256]{0:T(256)} %depth_h.3, f32[3]{0:T(128)} %b3_h.3, f32[128,1024]{1,0:T(8,128)S(1)} %get-tuple-element.18.east1, f32[128,1024]{1,0:T(8,128)S(1)} %get-tuple-element.19.north1, f32[128,1024]{1,0:T(8,128)S(1)} %get-tuple-element.20.tracer1, ...), custom_call_target="tpu_custom_call" | custom-call | tf_op jit(solution)/shard_map/second/pallas_call | solution.py:730
